TPU v7x, 512 devices: a whole 4x4x16 slice. The times are simulated.
512 devices in a mesh: seq: 128 (over x, z, core), head: 4 (over y).
Axes of the slice: x: 4, y: 4, z: 16, core: 2. Of those that a mesh axis runs over, the one named last changes fastest.
Arguments:
- queries: bfloat16 [16384, 2048], P('seq', 'head'), may hold values from -8 to 8
- keys: bfloat16 [16384, 2048], P('seq', 'head'), may hold values from -6 to 6
- values: bfloat16 [16384, 2048], P('seq', 'head'), may hold values from -18 to 18
- out_grad: bfloat16 [16384, 2048], P('seq', 'head'), may hold values from -6 to 6
- level_choice: int32 [128, 4], P('seq'), may hold values from 1 to 2
- frame_lengths: int32 [64], replicated, may hold values from 1 to 512, 16384 in all
Outputs:
- attended: bfloat16 [16384, 2048], P('seq', 'head')
- query_grad: bfloat16 [16384, 2048], P('seq', 'head')
- key_grad: bfloat16 [16384, 2048], P('seq', 'head')
- value_grad: bfloat16 [16384, 2048], P('seq', 'head')
Inputs may be any that keep to these rules, and one draw needn't show every extreme that they name: `frame_lengths`: the lengths sum to 16384.
All inputs are finite; a program needn't handle non-finite values.
Results may differ from a plain program's by a relative error of at most 0.025.
Values may be sent and summed in bfloat16 or wider, within the bound.
A program may use at most 64 MiB of HBM per device.

v0:
```python
import math

import jax
import jax.numpy as jnp
import numpy as np
from jax import lax
from jax.sharding import PartitionSpec as P

HEADS = 16
HEAD_DIM = 128
POOL1 = 4
POOL2 = 16
REACH1 = 3
REACH2 = 11


MATCHED_FRAME_ADD = 1.0
NORM_EPSILON = 1e-06


def extended(array, sides, width):
    for axis, dim in sides:
        size, length = (lax.axis_size(axis), array.shape[dim])
        up = [(i, (i + 1) % size) for i in range(size - 1)]
        down = [(j, i) for i, j in up]
        last = lax.slice_in_dim(array, length - width, length, axis=dim)
        leading = lax.slice_in_dim(array, 0, width, axis=dim)
        before = lax.ppermute(last, axis, up)
        after = lax.ppermute(leading, axis, down)
        array = jnp.concatenate([before, array, after], axis=dim)
    return array


def passed_along(block, axis, distance):
    devices = range(lax.axis_size(axis))
    route = [(i - distance, i) for i in devices if i - distance in devices]
    return lax.ppermute(block, axis, route)


def pool_rows(pair, factor):
    count = pair.shape[1] // factor
    grouped = pair.astype(jnp.float32).reshape(pair.shape[0], count, factor, pair.shape[2])
    return jnp.mean(grouped, axis=2).astype(jnp.bfloat16)


def spread_rows(total, factor):
    shape = (total.shape[0], total.shape[1], factor, total.shape[2])
    return jnp.broadcast_to(total[:, :, None, :] / factor, shape).reshape(
        total.shape[0], -1, total.shape[2]
    )


def frames_at(positions, frame_lengths):
    ends = jnp.cumsum(frame_lengths, dtype=jnp.int32)
    return jnp.sum((positions[:, None] >= ends[None, :]).astype(jnp.int32), axis=1, dtype=jnp.int32)


def frame_bias(query_frame_index, key_frame_index, valid):
    matched_frame = (query_frame_index[:, None] == key_frame_index[None, :]).astype(
        jnp.float32
    ) * MATCHED_FRAME_ADD
    return jnp.where(valid, matched_frame, -jnp.inf)


def by_heads(array, heads):
    return array.reshape(array.shape[0], heads, -1).transpose(1, 0, 2)


def from_heads(array):
    return array.transpose(1, 0, 2).reshape(array.shape[1], -1)


def contract(left, right):
    return lax.dot_general(
        left, right, (((1,), (1,)), ((), ())), preferred_element_type=jnp.float32
    )


def across(left, right):
    return lax.dot_general(
        left, right, (((0,), (0,)), ((), ())), preferred_element_type=jnp.float32
    )


def scores_of(query, key_rows, bias):
    return contract(query, key_rows) * (1.0 / math.sqrt(query.shape[1])) + bias


def head_forward_pass(query, key_rows, value_rows, bias):
    scores = scores_of(query, key_rows, bias)
    highest = jnp.max(scores, axis=1, keepdims=True)
    logsum = highest + jnp.log(jnp.sum(jnp.exp(scores - highest), axis=1, keepdims=True))
    rounded = jnp.exp(scores - logsum).astype(jnp.bfloat16)
    return (jnp.dot(rounded, value_rows, preferred_element_type=jnp.float32), logsum[:, 0])


def head_backward(query, mixed_grad, key_rows, value_rows, bias, logsum, delta):
    scale = 1.0 / math.sqrt(query.shape[1])
    weights = jnp.exp(scores_of(query, key_rows, bias) - logsum[:, None])
    rounded = weights.astype(jnp.bfloat16)
    slopes = (weights * (contract(mixed_grad, value_rows) - delta[:, None])).astype(jnp.bfloat16)
    query_grad = (jnp.dot(slopes, key_rows, preferred_element_type=jnp.float32) * scale).astype(
        jnp.bfloat16
    )
    key_grad = across(slopes, query) * scale
    value_grad = across(rounded, mixed_grad)
    return (query_grad, key_grad, value_grad)


def body(queries, keys, values, out_grad, level_choice, frame_lengths):
    rows, width = queries.shape
    heads = width // HEAD_DIM
    blocks = lax.axis_size("seq")
    place = lax.axis_index("seq")
    first_rows = rows // POOL1
    second_rows = rows // POOL2
    offsets_one = [offset for offset in range(-REACH1, REACH1 + 1) if abs(offset) >= 2]
    offsets_two = [offset for offset in range(-REACH2, REACH2 + 1) if abs(offset) >= 2]
    pair = jnp.stack([keys, values])
    first = pool_rows(pair, POOL1)
    second = pool_rows(pair, POOL2)
    near = extended(pair, (("seq", 1),), rows)
    first_far = jnp.stack([passed_along(first, "seq", -offset) for offset in offsets_one])
    second_far = jnp.stack([passed_along(second, "seq", -offset) for offset in offsets_two])
    positions = place * rows + jnp.arange(rows, dtype=jnp.int32)
    own_frame = frames_at(positions, frame_lengths)
    left_frame = frames_at(positions - rows, frame_lengths)
    right_frame = frames_at(positions + rows, frame_lengths)
    table = level_choice[0]
    blocks_one = place + jnp.array(offsets_one, dtype=jnp.int32)
    usable_one = (blocks_one >= 0) & (blocks_one < blocks) & (table == 1)
    blocks_two = place + jnp.array(offsets_two, dtype=jnp.int32)
    columns = np.array(
        [offsets_one.index(offset) if abs(offset) <= REACH1 else 0 for offset in offsets_two]
    )
    beyond = np.array([abs(offset) > REACH1 for offset in offsets_two])
    usable_two = (blocks_two >= 0) & (blocks_two < blocks) & (beyond | (table[columns] == 2))
    far_row = jnp.concatenate(
        [
            jnp.repeat(
                jnp.where(usable_one, math.log(POOL1), -jnp.inf).astype(jnp.float32), first_rows
            ),
            jnp.repeat(
                jnp.where(usable_two, math.log(POOL2), -jnp.inf).astype(jnp.float32), second_rows
            ),
        ]
    )
    bias = jnp.concatenate(
        [
            frame_bias(own_frame, own_frame, True),
            jnp.broadcast_to(far_row[None, :], (rows, far_row.shape[0])),
            frame_bias(own_frame, left_frame, place > 0),
            frame_bias(own_frame, right_frame, place < blocks - 1),
        ],
        axis=1,
    )
    gathered = jnp.concatenate(
        [
            pair,
            first_far.transpose(1, 0, 2, 3).reshape(2, -1, width),
            second_far.transpose(1, 0, 2, 3).reshape(2, -1, width),
            near[:, :rows],
            near[:, 2 * rows :],
        ],
        axis=1,
    )
    total = gathered.shape[1]
    tail = total - 2 * rows
    query_heads = by_heads(queries, heads)
    key_heads = by_heads(gathered[0], heads)
    value_heads = by_heads(gathered[1], heads)

    def forward_head(items):
        return head_forward_pass(items[0], items[1], items[2], bias)

    mixed_heads, logsum = lax.map(forward_head, (query_heads, key_heads, value_heads))
    mixed = from_heads(mixed_heads)
    energy = lax.psum(jnp.sum(mixed * mixed, axis=1), "head")
    inverse = lax.rsqrt(energy / (HEADS * HEAD_DIM) + NORM_EPSILON)[:, None]
    normed = mixed * inverse
    attended = normed.astype(jnp.bfloat16)
    incoming = out_grad.astype(jnp.float32)
    agreement = lax.psum(jnp.sum(incoming * normed, axis=1), "head")
    mixed_grad = (inverse * (incoming - normed * (agreement[:, None] / (HEADS * HEAD_DIM)))).astype(
        jnp.bfloat16
    )
    delta = jnp.sum((mixed_grad.astype(jnp.float32) * mixed).reshape(rows, heads, -1), axis=2).T

    def backward_head(items):
        return head_backward(items[0], items[1], items[2], items[3], bias, items[4], items[5])

    query_grad_heads, key_set, value_set = lax.map(
        backward_head,
        (query_heads, by_heads(mixed_grad, heads), key_heads, value_heads, logsum, delta),
    )
    set_grads = jnp.stack([from_heads(key_set), from_heads(value_set)])
    own_grad = set_grads[:, :rows]
    split_one = rows + len(offsets_one) * first_rows
    one_grad = (
        set_grads[:, rows:split_one]
        .reshape(2, len(offsets_one), first_rows, width)
        .transpose(1, 0, 2, 3)
    )
    two_grad = (
        set_grads[:, split_one:tail]
        .reshape(2, len(offsets_two), second_rows, width)
        .transpose(1, 0, 2, 3)
    )
    returned = [
        passed_along(
            set_grads[:, tail + index * rows : tail + (index + 1) * rows], "seq", directed_towards
        )
        for index, directed_towards in ((0, -1), (1, 1))
    ]
    own_grad = own_grad + returned[0] + returned[1]
    one_total = sum(
        [
            passed_along(one_grad[index].astype(jnp.bfloat16), "seq", offset).astype(jnp.float32)
            for index, offset in enumerate(offsets_one)
        ]
    )
    two_total = sum(
        [
            passed_along(two_grad[index].astype(jnp.bfloat16), "seq", offset).astype(jnp.float32)
            for index, offset in enumerate(offsets_two)
        ]
    )
    token_grad = (own_grad + spread_rows(one_total, POOL1) + spread_rows(two_total, POOL2)).astype(
        jnp.bfloat16
    )
    return (attended, from_heads(query_grad_heads), token_grad[0], token_grad[1])


def solution(mesh):
    in_specs = (
        P("seq", "head"),
        P("seq", "head"),
        P("seq", "head"),
        P("seq", "head"),
        P("seq", None),
        P(),
    )
    out_specs = (P("seq", "head"), P("seq", "head"), P("seq", "head"), P("seq", "head"))
    return jax.shard_map(body, mesh=mesh, in_specs=in_specs, out_specs=out_specs, check_vma=False)
```

profile of v0, /device:TPU:6, one launch (start us, length us, event | category | flops | bytes accessed | tf_op | source)
XLA Modules:
  0.0 358.5 jit_solution(23133626604398621)
XLA Ops:
  1.8 14.5 %collective-permute-start.23 = (bf16[2,8,512]{2,1,0:T(8,128)(2,1)S(1)}, bf16[2,8,512]{2,1,0:T(8,128)(2,1)S(1)}, u32[]{:S(2)}, u32[]{:S(2)}) collective-permute-start(bf16[2,8,512]{2,1,0:T(8,128)(2,1)S(1)} %multiply_convert_fusion.1), channel_id=1, source_target_pairs={{44,0},{48,4},{52,8},{56,12},{60,16},{64,20},{68,24},{72,28},{76,3... | collective-permute-start | bytes 49160 | tf_op jit(solution)/shard_map/ppermute | solution.py:37
  21.0 9.8 %collective-permute-start.20 = (bf16[2,8,512]{2,1,0:T(8,128)(2,1)S(1)}, bf16[2,8,512]{2,1,0:T(8,128)(2,1)S(1)}, u32[]{:S(2)}, u32[]{:S(2)}) collective-permute-start(bf16[2,8,512]{2,1,0:T(8,128)(2,1)S(1)} %multiply_convert_fusion.1), channel_id=1, source_target_pairs={{32,0},{36,4},{40,8},{44,12},{48,16},{52,20},{56,24},{60,28},{64,3... | collective-permute-start | bytes 49160 | tf_op jit(solution)/shard_map/ppermute | solution.py:37
  43.7 6.8 %collective-permute-start.5 = (bf16[2,8,512]{2,1,0:T(8,128)(2,1)S(1)}, bf16[2,8,512]{2,1,0:T(8,128)(2,1)S(1)}, u32[]{:S(2)}, u32[]{:S(2)}) collective-permute-start(bf16[2,8,512]{2,1,0:T(8,128)(2,1)S(1)} %multiply_convert_fusion.1), channel_id=1, source_target_pairs={{0,40},{4,44},{8,48},{12,52},{16,56},{20,60},{24,64},{28,68},{32,7... | collective-permute-start | bytes 49160 | tf_op jit(solution)/shard_map/ppermute | solution.py:37
  50.6 5.9 %collective-permute-done.5 = bf16[2,8,512]{2,1,0:T(8,128)(2,1)S(1)} collective-permute-done((bf16[2,8,512]{2,1,0:T(8,128)(2,1)S(1)}, bf16[2,8,512]{2,1,0:T(8,128)(2,1)S(1)}, u32[]{:S(2)}, u32[]{:S(2)}) %collective-permute-start.5) | collective-permute-done | bytes 16416 | tf_op jit(solution)/shard_map/ppermute | solution.py:37
  56.5 6.0 %collective-permute-start.6 = (bf16[2,8,512]{2,1,0:T(8,128)(2,1)S(1)}, bf16[2,8,512]{2,1,0:T(8,128)(2,1)S(1)}, u32[]{:S(2)}, u32[]{:S(2)}) collective-permute-start(bf16[2,8,512]{2,1,0:T(8,128)(2,1)S(1)} %multiply_convert_fusion.1), channel_id=1, source_target_pairs={{0,36},{4,40},{8,44},{12,48},{16,52},{20,56},{24,60},{28,64},{32,6... | collective-permute-start | bytes 49160 | tf_op jit(solution)/shard_map/ppermute | solution.py:37
  62.5 6.0 %collective-permute-done.6 = bf16[2,8,512]{2,1,0:T(8,128)(2,1)S(1)} collective-permute-done((bf16[2,8,512]{2,1,0:T(8,128)(2,1)S(1)}, bf16[2,8,512]{2,1,0:T(8,128)(2,1)S(1)}, u32[]{:S(2)}, u32[]{:S(2)}) %collective-permute-start.6) | collective-permute-done | bytes 16416 | tf_op jit(solution)/shard_map/ppermute | solution.py:37
  68.4 5.3 %collective-permute-start.7 = (bf16[2,8,512]{2,1,0:T(8,128)(2,1)S(1)}, bf16[2,8,512]{2,1,0:T(8,128)(2,1)S(1)}, u32[]{:S(2)}, u32[]{:S(2)}) collective-permute-start(bf16[2,8,512]{2,1,0:T(8,128)(2,1)S(1)} %multiply_convert_fusion.1), channel_id=1, source_target_pairs={{0,32},{4,36},{8,40},{12,44},{16,48},{20,52},{24,56},{28,60},{32,6... | collective-permute-start | bytes 49160 | tf_op jit(solution)/shard_map/ppermute | solution.py:37
  73.8 5.3 %collective-permute-done.7 = bf16[2,8,512]{2,1,0:T(8,128)(2,1)S(1)} collective-permute-done((bf16[2,8,512]{2,1,0:T(8,128)(2,1)S(1)}, bf16[2,8,512]{2,1,0:T(8,128)(2,1)S(1)}, u32[]{:S(2)}, u32[]{:S(2)}) %collective-permute-start.7) | collective-permute-done | bytes 16416 | tf_op jit(solution)/shard_map/ppermute | solution.py:37
  81.0 7.9 %collective-permute-done.8 = bf16[2,8,512]{2,1,0:T(8,128)(2,1)S(1)} collective-permute-done((bf16[2,8,512]{2,1,0:T(8,128)(2,1)S(1)}, bf16[2,8,512]{2,1,0:T(8,128)(2,1)S(1)}, u32[]{:S(2)}, u32[]{:S(2)}) %collective-permute-start.8) | collective-permute-done | bytes 16416 | tf_op jit(solution)/shard_map/ppermute | solution.py:37
  91.2 7.2 %collective-permute-done.9 = bf16[2,8,512]{2,1,0:T(8,128)(2,1)S(1)} collective-permute-done((bf16[2,8,512]{2,1,0:T(8,128)(2,1)S(1)}, bf16[2,8,512]{2,1,0:T(8,128)(2,1)S(1)}, u32[]{:S(2)}, u32[]{:S(2)}) %collective-permute-start.9) | collective-permute-done | bytes 16416 | tf_op jit(solution)/shard_map/ppermute | solution.py:37
  100.4 7.0 %collective-permute-done.10 = bf16[2,8,512]{2,1,0:T(8,128)(2,1)S(1)} collective-permute-done((bf16[2,8,512]{2,1,0:T(8,128)(2,1)S(1)}, bf16[2,8,512]{2,1,0:T(8,128)(2,1)S(1)}, u32[]{:S(2)}, u32[]{:S(2)}) %collective-permute-start.10) | collective-permute-done | bytes 16416 | tf_op jit(solution)/shard_map/ppermute | solution.py:37
  109.3 6.7 %collective-permute-done.11 = bf16[2,8,512]{2,1,0:T(8,128)(2,1)S(1)} collective-permute-done((bf16[2,8,512]{2,1,0:T(8,128)(2,1)S(1)}, bf16[2,8,512]{2,1,0:T(8,128)(2,1)S(1)}, u32[]{:S(2)}, u32[]{:S(2)}) %collective-permute-start.11) | collective-permute-done | bytes 16416 | tf_op jit(solution)/shard_map/ppermute | solution.py:37
  117.9 6.1 %collective-permute-done.12 = bf16[2,8,512]{2,1,0:T(8,128)(2,1)S(1)} collective-permute-done((bf16[2,8,512]{2,1,0:T(8,128)(2,1)S(1)}, bf16[2,8,512]{2,1,0:T(8,128)(2,1)S(1)}, u32[]{:S(2)}, u32[]{:S(2)}) %collective-permute-start.12) | collective-permute-done | bytes 16416 | tf_op jit(solution)/shard_map/ppermute | solution.py:37
  126.0 5.8 %collective-permute-done.13 = bf16[2,8,512]{2,1,0:T(8,128)(2,1)S(1)} collective-permute-done((bf16[2,8,512]{2,1,0:T(8,128)(2,1)S(1)}, bf16[2,8,512]{2,1,0:T(8,128)(2,1)S(1)}, u32[]{:S(2)}, u32[]{:S(2)}) %collective-permute-start.13) | collective-permute-done | bytes 16416 | tf_op jit(solution)/shard_map/ppermute | solution.py:37
  144.4 4.6 %collective-permute-done.16 = bf16[2,8,512]{2,1,0:T(8,128)(2,1)S(1)} collective-permute-done((bf16[2,8,512]{2,1,0:T(8,128)(2,1)S(1)}, bf16[2,8,512]{2,1,0:T(8,128)(2,1)S(1)}, u32[]{:S(2)}, u32[]{:S(2)}) %collective-permute-start.16) | collective-permute-done | bytes 16416 | tf_op jit(solution)/shard_map/ppermute | solution.py:37
  154.9 5.6 %collective-permute-start.18 = (bf16[2,8,512]{2,1,0:T(8,128)(2,1)S(1)}, bf16[2,8,512]{2,1,0:T(8,128)(2,1)S(1)}, u32[]{:S(2)}, u32[]{:S(2)}) collective-permute-start(bf16[2,8,512]{2,1,0:T(8,128)(2,1)S(1)} %multiply_convert_fusion.1), channel_id=1, source_target_pairs={{24,0},{28,4},{32,8},{36,12},{40,16},{44,20},{48,24},{52,28},{56,3... | collective-permute-start | bytes 49160 | tf_op jit(solution)/shard_map/ppermute | solution.py:37
  162.4 7.4 %collective-permute-start.19 = (bf16[2,8,512]{2,1,0:T(8,128)(2,1)S(1)}, bf16[2,8,512]{2,1,0:T(8,128)(2,1)S(1)}, u32[]{:S(2)}, u32[]{:S(2)}) collective-permute-start(bf16[2,8,512]{2,1,0:T(8,128)(2,1)S(1)} %multiply_convert_fusion.1), channel_id=1, source_target_pairs={{28,0},{32,4},{36,8},{40,12},{44,16},{48,20},{52,24},{56,28},{60,3... | collective-permute-start | bytes 49160 | tf_op jit(solution)/shard_map/ppermute | solution.py:37
  171.2 10.8 %collective-permute-start.3 = (bf16[2,32,512]{2,1,0:T(8,128)(2,1)S(1)}, bf16[2,32,512]{2,1,0:T(8,128)(2,1)S(1)}, u32[]{:S(2)}, u32[]{:S(2)}) collective-permute-start(bf16[2,32,512]{2,1,0:T(8,128)(2,1)S(1)} %multiply_convert_fusion), channel_id=1, source_target_pairs={{12,0},{16,4},{20,8},{24,12},{28,16},{32,20},{36,24},{40,28},{44,3... | collective-permute-start | bytes 196616 | tf_op jit(solution)/shard_map/ppermute | solution.py:37
  193.2 5.6 %collective-permute-start.25 = (bf16[2,128,512]{2,1,0:T(8,128)(2,1)S(1)}, bf16[2,128,512]{2,1,0:T(8,128)(2,1)S(1)}, u32[]{:S(2)}, u32[]{:S(2)}) collective-permute-start(bf16[2,128,512]{2,1,0:T(8,128)(2,1)S(1)} %get-tuple-element.253), channel_id=1, source_target_pairs={{4,0},{8,4},{12,8},{16,12},{20,16},{24,20},{28,24},{32,28},{36,32}... | collective-permute-start | bytes 786440 | tf_op jit(solution)/shard_map/ppermute | solution.py:29
  208.4 10.8 %psum.14 = f32[128]{0:T(128)S(1)} all-reduce(f32[128]{0:T(128)S(1)} %fusion.52), channel_id=1, replica_groups=mesh['seq'=128,'head'=4] {'head'}, use_global_device_ids=true, to_apply=%region_11.12 | all-reduce | flops 128 | bytes 1024 | tf_op jit(solution)/shard_map/psum | solution.py:178
  219.3 7.7 %psum.15 = f32[128]{0:T(128)S(1)} all-reduce(f32[128]{0:T(128)S(1)} %fusion.49), channel_id=1, replica_groups=mesh['seq'=128,'head'=4] {'head'}, use_global_device_ids=true, to_apply=%region_13.14 | all-reduce | flops 128 | bytes 1024 | tf_op jit(solution)/shard_map/psum | solution.py:183
  228.3 10.4 %while.27 = (s32[]{:T(128)}, bf16[4,128,128]{2,1,0:T(8,128)(2,1)S(1)}, f32[4,672,128]{2,1,0:T(8,128)}, f32[4,672,128]{2,1,0:T(8,128)}, bf16[4,128,128]{2,1,0:T(8...) while((s32[]{:T(128)}, ...), condition=%wide.region_16.17_spmd, body=%wide.region_15.16_spmd.sunk | while | flops 110821376 | bytes 3268737 | solution.py:192
  248.9 8.4 %collective-permute-start.51 = (bf16[2,8,512]{2,1,0:T(8,128)(2,1)S(1)}, bf16[2,8,512]{2,1,0:T(8,128)(2,1)S(1)}, u32[]{:S(2)}, u32[]{:S(2)}) collective-permute-start(bf16[2,8,512]{2,1,0:T(8,128)(2,1)S(1)} %get-tuple-element.228), channel_id=1, source_target_pairs={{0,44},{4,48},{8,52},{12,56},{16,60},{20,64},{24,68},{28,72},{32,7... | collective-permute-start | bytes 49160 | tf_op jit(solution)/shard_map/ppermute | solution.py:37
  279.3 5.8 %collective-permute-start.41 = (bf16[2,8,512]{2,1,0:T(8,128)(2,1)S(1)}, bf16[2,8,512]{2,1,0:T(8,128)(2,1)S(1)}, u32[]{:S(2)}, u32[]{:S(2)}) collective-permute-start(bf16[2,8,512]{2,1,0:T(8,128)(2,1)S(1)} %get-tuple-element.238), channel_id=1, source_target_pairs={{8,0},{12,4},{16,8},{20,12},{24,16},{28,20},{32,24},{36,28},{40,32... | collective-permute-start | bytes 49160 | tf_op jit(solution)/shard_map/ppermute | solution.py:37
  289.2 5.0 %collective-permute-start.39 = (bf16[2,8,512]{2,1,0:T(8,128)(2,1)S(1)}, bf16[2,8,512]{2,1,0:T(8,128)(2,1)S(1)}, u32[]{:S(2)}, u32[]{:S(2)}) collective-permute-start(bf16[2,8,512]{2,1,0:T(8,128)(2,1)S(1)} %get-tuple-element.240), channel_id=1, source_target_pairs={{16,0},{20,4},{24,8},{28,12},{32,16},{36,20},{40,24},{44,28},{48,3... | collective-permute-start | bytes 49160 | tf_op jit(solution)/shard_map/ppermute | solution.py:37
  294.1 4.4 %collective-permute-start.38 = (bf16[2,8,512]{2,1,0:T(8,128)(2,1)S(1)}, bf16[2,8,512]{2,1,0:T(8,128)(2,1)S(1)}, u32[]{:S(2)}, u32[]{:S(2)}) collective-permute-start(bf16[2,8,512]{2,1,0:T(8,128)(2,1)S(1)} %get-tuple-element.241), channel_id=1, source_target_pairs={{20,0},{24,4},{28,8},{32,12},{36,16},{40,20},{44,24},{48,28},{52,3... | collective-permute-start | bytes 49160 | tf_op jit(solution)/shard_map/ppermute | solution.py:37
  298.6 4.3 %collective-permute-start.37 = (bf16[2,8,512]{2,1,0:T(8,128)(2,1)S(1)}, bf16[2,8,512]{2,1,0:T(8,128)(2,1)S(1)}, u32[]{:S(2)}, u32[]{:S(2)}) collective-permute-start(bf16[2,8,512]{2,1,0:T(8,128)(2,1)S(1)} %get-tuple-element.242), channel_id=1, source_target_pairs={{24,0},{28,4},{32,8},{36,12},{40,16},{44,20},{48,24},{52,28},{56,3... | collective-permute-start | bytes 49160 | tf_op jit(solution)/shard_map/ppermute | solution.py:37
  302.9 7.0 %collective-permute-start.36 = (bf16[2,8,512]{2,1,0:T(8,128)(2,1)S(1)}, bf16[2,8,512]{2,1,0:T(8,128)(2,1)S(1)}, u32[]{:S(2)}, u32[]{:S(2)}) collective-permute-start(bf16[2,8,512]{2,1,0:T(8,128)(2,1)S(1)} %get-tuple-element.243), channel_id=1, source_target_pairs={{28,0},{32,4},{36,8},{40,12},{44,16},{48,20},{52,24},{56,28},{60,3... | collective-permute-start | bytes 49160 | tf_op jit(solution)/shard_map/ppermute | solution.py:37
  309.9 8.8 %collective-permute-start.35 = (bf16[2,8,512]{2,1,0:T(8,128)(2,1)S(1)}, bf16[2,8,512]{2,1,0:T(8,128)(2,1)S(1)}, u32[]{:S(2)}, u32[]{:S(2)}) collective-permute-start(bf16[2,8,512]{2,1,0:T(8,128)(2,1)S(1)} %get-tuple-element.244), channel_id=1, source_target_pairs={{32,0},{36,4},{40,8},{44,12},{48,16},{52,20},{56,24},{60,28},{64,3... | collective-permute-start | bytes 49160 | tf_op jit(solution)/shard_map/ppermute | solution.py:37
  322.1 8.4 %collective-permute-start.34 = (bf16[2,8,512]{2,1,0:T(8,128)(2,1)S(1)}, bf16[2,8,512]{2,1,0:T(8,128)(2,1)S(1)}, u32[]{:S(2)}, u32[]{:S(2)}) collective-permute-start(bf16[2,8,512]{2,1,0:T(8,128)(2,1)S(1)} %get-tuple-element.245), channel_id=1, source_target_pairs={{36,0},{40,4},{44,8},{48,12},{52,16},{56,20},{60,24},{64,28},{68,3... | collective-permute-start | bytes 49160 | tf_op jit(solution)/shard_map/ppermute | solution.py:37
  330.5 7.5 %collective-permute-start.33 = (bf16[2,8,512]{2,1,0:T(8,128)(2,1)S(1)}, bf16[2,8,512]{2,1,0:T(8,128)(2,1)S(1)}, u32[]{:S(2)}, u32[]{:S(2)}) collective-permute-start(bf16[2,8,512]{2,1,0:T(8,128)(2,1)S(1)} %slice_bitcast_fusion.24), channel_id=1, source_target_pairs={{40,0},{44,4},{48,8},{52,12},{56,16},{60,20},{64,24},{68,28},{72,3... | collective-permute-start | bytes 49160 | tf_op jit(solution)/shard_map/ppermute | solution.py:37
  348.7 5.5 %collective-permute-start.29 = (bf16[2,32,512]{2,1,0:T(8,128)(2,1)S(1)}, bf16[2,32,512]{2,1,0:T(8,128)(2,1)S(1)}, u32[]{:S(2)}, u32[]{:S(2)}) collective-permute-start(bf16[2,32,512]{2,1,0:T(8,128)(2,1)S(1)} %get-tuple-element.252), channel_id=1, source_target_pairs={{8,0},{12,4},{16,8},{20,12},{24,16},{28,20},{32,24},{36,28},{40,32... | collective-permute-start | bytes 196616 | tf_op jit(solution)/shard_map/ppermute | solution.py:37
  (220 shorter events, 141.3 us)
Async XLA Ops:
  1.8 189.4 %collective-permute-start.23 = (bf16[2,8,512]{2,1,0:T(8,128)(2,1)S(1)}, bf16[2,8,512]{2,1,0:T(8,128)(2,1)S(1)}, u32[]{:S(2)}, u32[]{:S(2)}) collective-permute-start(bf16[2,8,512]{2,1,0:T(8,128)(2,1)S(1)} %multiply_convert_fusion.1), channel_id=1, source_target_pairs={{44,0},{48,4},{52,8},{56,12},{60,16},{64,20},{68,24},{72,28},{76,3... | collective-permute-start | bytes 49160 | tf_op jit(solution)/shard_map/ppermute | solution.py:37
  16.3 171.7 %collective-permute-start.22 = (bf16[2,8,512]{2,1,0:T(8,128)(2,1)S(1)}, bf16[2,8,512]{2,1,0:T(8,128)(2,1)S(1)}, u32[]{:S(2)}, u32[]{:S(2)}) collective-permute-start(bf16[2,8,512]{2,1,0:T(8,128)(2,1)S(1)} %multiply_convert_fusion.1), channel_id=1, source_target_pairs={{40,0},{44,4},{48,8},{52,12},{56,16},{60,20},{64,24},{68,28},{72,3... | collective-permute-start | bytes 49160 | tf_op jit(solution)/shard_map/ppermute | solution.py:37
  18.4 167.4 %collective-permute-start.21 = (bf16[2,8,512]{2,1,0:T(8,128)(2,1)S(1)}, bf16[2,8,512]{2,1,0:T(8,128)(2,1)S(1)}, u32[]{:S(2)}, u32[]{:S(2)}) collective-permute-start(bf16[2,8,512]{2,1,0:T(8,128)(2,1)S(1)} %multiply_convert_fusion.1), channel_id=1, source_target_pairs={{36,0},{40,4},{44,8},{48,12},{52,16},{56,20},{60,24},{64,28},{68,3... | collective-permute-start | bytes 49160 | tf_op jit(solution)/shard_map/ppermute | solution.py:37
  21.0 161.1 %collective-permute-start.20 = (bf16[2,8,512]{2,1,0:T(8,128)(2,1)S(1)}, bf16[2,8,512]{2,1,0:T(8,128)(2,1)S(1)}, u32[]{:S(2)}, u32[]{:S(2)}) collective-permute-start(bf16[2,8,512]{2,1,0:T(8,128)(2,1)S(1)} %multiply_convert_fusion.1), channel_id=1, source_target_pairs={{32,0},{36,4},{40,8},{44,12},{48,16},{52,20},{56,24},{60,28},{64,3... | collective-permute-start | bytes 49160 | tf_op jit(solution)/shard_map/ppermute | solution.py:37
  30.8 12.9 %collective-permute-start.4 = (bf16[2,8,512]{2,1,0:T(8,128)(2,1)S(1)}, bf16[2,8,512]{2,1,0:T(8,128)(2,1)S(1)}, u32[]{:S(2)}, u32[]{:S(2)}) collective-permute-start(bf16[2,8,512]{2,1,0:T(8,128)(2,1)S(1)} %multiply_convert_fusion.1), channel_id=1, source_target_pairs={{0,44},{4,48},{8,52},{12,56},{16,60},{20,64},{24,68},{28,72},{32,7... | collective-permute-start | bytes 49160 | tf_op jit(solution)/shard_map/ppermute | solution.py:37
  43.7 12.8 %collective-permute-start.5 = (bf16[2,8,512]{2,1,0:T(8,128)(2,1)S(1)}, bf16[2,8,512]{2,1,0:T(8,128)(2,1)S(1)}, u32[]{:S(2)}, u32[]{:S(2)}) collective-permute-start(bf16[2,8,512]{2,1,0:T(8,128)(2,1)S(1)} %multiply_convert_fusion.1), channel_id=1, source_target_pairs={{0,40},{4,44},{8,48},{12,52},{16,56},{20,60},{24,64},{28,68},{32,7... | collective-permute-start | bytes 49160 | tf_op jit(solution)/shard_map/ppermute | solution.py:37
  171.2 22.0 %collective-permute-start.3 = (bf16[2,32,512]{2,1,0:T(8,128)(2,1)S(1)}, bf16[2,32,512]{2,1,0:T(8,128)(2,1)S(1)}, u32[]{:S(2)}, u32[]{:S(2)}) collective-permute-start(bf16[2,32,512]{2,1,0:T(8,128)(2,1)S(1)} %multiply_convert_fusion), channel_id=1, source_target_pairs={{12,0},{16,4},{20,8},{24,12},{28,16},{32,20},{36,24},{40,28},{44,3... | collective-permute-start | bytes 196616 | tf_op jit(solution)/shard_map/ppermute | solution.py:37
  182.1 16.8 %collective-permute-start.2 = (bf16[2,32,512]{2,1,0:T(8,128)(2,1)S(1)}, bf16[2,32,512]{2,1,0:T(8,128)(2,1)S(1)}, u32[]{:S(2)}, u32[]{:S(2)}) collective-permute-start(bf16[2,32,512]{2,1,0:T(8,128)(2,1)S(1)} %multiply_convert_fusion), channel_id=1, source_target_pairs={{8,0},{12,4},{16,8},{20,12},{24,16},{28,20},{32,24},{36,28},{40,32... | collective-permute-start | bytes 196616 | tf_op jit(solution)/shard_map/ppermute | solution.py:37
  185.8 13.1 %collective-permute-start.1 = (bf16[2,32,512]{2,1,0:T(8,128)(2,1)S(1)}, bf16[2,32,512]{2,1,0:T(8,128)(2,1)S(1)}, u32[]{:S(2)}, u32[]{:S(2)}) collective-permute-start(bf16[2,32,512]{2,1,0:T(8,128)(2,1)S(1)} %multiply_convert_fusion), channel_id=1, source_target_pairs={{0,8},{4,12},{8,16},{12,20},{16,24},{20,28},{24,32},{28,36},{32,40... | collective-permute-start | bytes 196616 | tf_op jit(solution)/shard_map/ppermute | solution.py:37
  247.0 16.4 %collective-permute-start.32 = (bf16[2,8,512]{2,1,0:T(8,128)(2,1)S(1)}, bf16[2,8,512]{2,1,0:T(8,128)(2,1)S(1)}, u32[]{:S(2)}, u32[]{:S(2)}) collective-permute-start(bf16[2,8,512]{2,1,0:T(8,128)(2,1)S(1)} %get-tuple-element.227), channel_id=1, source_target_pairs={{44,0},{48,4},{52,8},{56,12},{60,16},{64,20},{68,24},{72,28},{76,3... | collective-permute-start | bytes 49160 | tf_op jit(solution)/shard_map/ppermute | solution.py:37
  248.9 16.5 %collective-permute-start.51 = (bf16[2,8,512]{2,1,0:T(8,128)(2,1)S(1)}, bf16[2,8,512]{2,1,0:T(8,128)(2,1)S(1)}, u32[]{:S(2)}, u32[]{:S(2)}) collective-permute-start(bf16[2,8,512]{2,1,0:T(8,128)(2,1)S(1)} %get-tuple-element.228), channel_id=1, source_target_pairs={{0,44},{4,48},{8,52},{12,56},{16,60},{20,64},{24,68},{28,72},{32,7... | collective-permute-start | bytes 49160 | tf_op jit(solution)/shard_map/ppermute | solution.py:37
  257.3 12.7 %collective-permute-start.50 = (bf16[2,8,512]{2,1,0:T(8,128)(2,1)S(1)}, bf16[2,8,512]{2,1,0:T(8,128)(2,1)S(1)}, u32[]{:S(2)}, u32[]{:S(2)}) collective-permute-start(bf16[2,8,512]{2,1,0:T(8,128)(2,1)S(1)} %get-tuple-element.229), channel_id=1, source_target_pairs={{0,40},{4,44},{8,48},{12,52},{16,56},{20,60},{24,64},{28,68},{32,7... | collective-permute-start | bytes 49160 | tf_op jit(solution)/shard_map/ppermute | solution.py:37
  259.5 12.7 %collective-permute-start.49 = (bf16[2,8,512]{2,1,0:T(8,128)(2,1)S(1)}, bf16[2,8,512]{2,1,0:T(8,128)(2,1)S(1)}, u32[]{:S(2)}, u32[]{:S(2)}) collective-permute-start(bf16[2,8,512]{2,1,0:T(8,128)(2,1)S(1)} %get-tuple-element.230), channel_id=1, source_target_pairs={{0,36},{4,40},{8,44},{12,48},{16,52},{20,56},{24,60},{28,64},{32,6... | collective-permute-start | bytes 49160 | tf_op jit(solution)/shard_map/ppermute | solution.py:37
  261.5 13.7 %collective-permute-start.48 = (bf16[2,8,512]{2,1,0:T(8,128)(2,1)S(1)}, bf16[2,8,512]{2,1,0:T(8,128)(2,1)S(1)}, u32[]{:S(2)}, u32[]{:S(2)}) collective-permute-start(bf16[2,8,512]{2,1,0:T(8,128)(2,1)S(1)} %get-tuple-element.231), channel_id=1, source_target_pairs={{0,32},{4,36},{8,40},{12,44},{16,48},{20,52},{24,56},{28,60},{32,6... | collective-permute-start | bytes 49160 | tf_op jit(solution)/shard_map/ppermute | solution.py:37
  263.4 13.7 %collective-permute-start.47 = (bf16[2,8,512]{2,1,0:T(8,128)(2,1)S(1)}, bf16[2,8,512]{2,1,0:T(8,128)(2,1)S(1)}, u32[]{:S(2)}, u32[]{:S(2)}) collective-permute-start(bf16[2,8,512]{2,1,0:T(8,128)(2,1)S(1)} %get-tuple-element.232), channel_id=1, source_target_pairs={{0,28},{4,32},{8,36},{12,40},{16,44},{20,48},{24,52},{28,56},{32,6... | collective-permute-start | bytes 49160 | tf_op jit(solution)/shard_map/ppermute | solution.py:37
  265.4 14.0 %collective-permute-start.46 = (bf16[2,8,512]{2,1,0:T(8,128)(2,1)S(1)}, bf16[2,8,512]{2,1,0:T(8,128)(2,1)S(1)}, u32[]{:S(2)}, u32[]{:S(2)}) collective-permute-start(bf16[2,8,512]{2,1,0:T(8,128)(2,1)S(1)} %get-tuple-element.233), channel_id=1, source_target_pairs={{0,24},{4,28},{8,32},{12,36},{16,40},{20,44},{24,48},{28,52},{32,5... | collective-permute-start | bytes 49160 | tf_op jit(solution)/shard_map/ppermute | solution.py:37
  270.0 15.1 %collective-permute-start.45 = (bf16[2,8,512]{2,1,0:T(8,128)(2,1)S(1)}, bf16[2,8,512]{2,1,0:T(8,128)(2,1)S(1)}, u32[]{:S(2)}, u32[]{:S(2)}) collective-permute-start(bf16[2,8,512]{2,1,0:T(8,128)(2,1)S(1)} %get-tuple-element.234), channel_id=1, source_target_pairs={{0,20},{4,24},{8,28},{12,32},{16,36},{20,40},{24,44},{28,48},{32,5... | collective-permute-start | bytes 49160 | tf_op jit(solution)/shard_map/ppermute | solution.py:37
  272.2 17.0 %collective-permute-start.44 = (bf16[2,8,512]{2,1,0:T(8,128)(2,1)S(1)}, bf16[2,8,512]{2,1,0:T(8,128)(2,1)S(1)}, u32[]{:S(2)}, u32[]{:S(2)}) collective-permute-start(bf16[2,8,512]{2,1,0:T(8,128)(2,1)S(1)} %get-tuple-element.235), channel_id=1, source_target_pairs={{0,16},{4,20},{8,24},{12,28},{16,32},{20,36},{24,40},{28,44},{32,4... | collective-permute-start | bytes 49160 | tf_op jit(solution)/shard_map/ppermute | solution.py:37
  275.2 19.0 %collective-permute-start.43 = (bf16[2,8,512]{2,1,0:T(8,128)(2,1)S(1)}, bf16[2,8,512]{2,1,0:T(8,128)(2,1)S(1)}, u32[]{:S(2)}, u32[]{:S(2)}) collective-permute-start(bf16[2,8,512]{2,1,0:T(8,128)(2,1)S(1)} %get-tuple-element.236), channel_id=1, source_target_pairs={{0,12},{4,16},{8,20},{12,24},{16,28},{20,32},{24,36},{28,40},{32,4... | collective-permute-start | bytes 49160 | tf_op jit(solution)/shard_map/ppermute | solution.py:37
  277.1 21.5 %collective-permute-start.42 = (bf16[2,8,512]{2,1,0:T(8,128)(2,1)S(1)}, bf16[2,8,512]{2,1,0:T(8,128)(2,1)S(1)}, u32[]{:S(2)}, u32[]{:S(2)}) collective-permute-start(bf16[2,8,512]{2,1,0:T(8,128)(2,1)S(1)} %get-tuple-element.237), channel_id=1, source_target_pairs={{0,8},{4,12},{8,16},{12,20},{16,24},{20,28},{24,32},{28,36},{32,40... | collective-permute-start | bytes 49160 | tf_op jit(solution)/shard_map/ppermute | solution.py:37
  279.3 23.5 %collective-permute-start.41 = (bf16[2,8,512]{2,1,0:T(8,128)(2,1)S(1)}, bf16[2,8,512]{2,1,0:T(8,128)(2,1)S(1)}, u32[]{:S(2)}, u32[]{:S(2)}) collective-permute-start(bf16[2,8,512]{2,1,0:T(8,128)(2,1)S(1)} %get-tuple-element.238), channel_id=1, source_target_pairs={{8,0},{12,4},{16,8},{20,12},{24,16},{28,20},{32,24},{36,28},{40,32... | collective-permute-start | bytes 49160 | tf_op jit(solution)/shard_map/ppermute | solution.py:37
  285.1 24.7 %collective-permute-start.40 = (bf16[2,8,512]{2,1,0:T(8,128)(2,1)S(1)}, bf16[2,8,512]{2,1,0:T(8,128)(2,1)S(1)}, u32[]{:S(2)}, u32[]{:S(2)}) collective-permute-start(bf16[2,8,512]{2,1,0:T(8,128)(2,1)S(1)} %get-tuple-element.239), channel_id=1, source_target_pairs={{12,0},{16,4},{20,8},{24,12},{28,16},{32,20},{36,24},{40,28},{44,3... | collective-permute-start | bytes 49160 | tf_op jit(solution)/shard_map/ppermute | solution.py:37
  289.2 29.5 %collective-permute-start.39 = (bf16[2,8,512]{2,1,0:T(8,128)(2,1)S(1)}, bf16[2,8,512]{2,1,0:T(8,128)(2,1)S(1)}, u32[]{:S(2)}, u32[]{:S(2)}) collective-permute-start(bf16[2,8,512]{2,1,0:T(8,128)(2,1)S(1)} %get-tuple-element.240), channel_id=1, source_target_pairs={{16,0},{20,4},{24,8},{28,12},{32,16},{36,20},{40,24},{44,28},{48,3... | collective-permute-start | bytes 49160 | tf_op jit(solution)/shard_map/ppermute | solution.py:37
  294.1 27.9 %collective-permute-start.38 = (bf16[2,8,512]{2,1,0:T(8,128)(2,1)S(1)}, bf16[2,8,512]{2,1,0:T(8,128)(2,1)S(1)}, u32[]{:S(2)}, u32[]{:S(2)}) collective-permute-start(bf16[2,8,512]{2,1,0:T(8,128)(2,1)S(1)} %get-tuple-element.241), channel_id=1, source_target_pairs={{20,0},{24,4},{28,8},{32,12},{36,16},{40,20},{44,24},{48,28},{52,3... | collective-permute-start | bytes 49160 | tf_op jit(solution)/shard_map/ppermute | solution.py:37
  298.6 31.9 %collective-permute-start.37 = (bf16[2,8,512]{2,1,0:T(8,128)(2,1)S(1)}, bf16[2,8,512]{2,1,0:T(8,128)(2,1)S(1)}, u32[]{:S(2)}, u32[]{:S(2)}) collective-permute-start(bf16[2,8,512]{2,1,0:T(8,128)(2,1)S(1)} %get-tuple-element.242), channel_id=1, source_target_pairs={{24,0},{28,4},{32,8},{36,12},{40,16},{44,20},{48,24},{52,28},{56,3... | collective-permute-start | bytes 49160 | tf_op jit(solution)/shard_map/ppermute | solution.py:37
  302.9 35.1 %collective-permute-start.36 = (bf16[2,8,512]{2,1,0:T(8,128)(2,1)S(1)}, bf16[2,8,512]{2,1,0:T(8,128)(2,1)S(1)}, u32[]{:S(2)}, u32[]{:S(2)}) collective-permute-start(bf16[2,8,512]{2,1,0:T(8,128)(2,1)S(1)} %get-tuple-element.243), channel_id=1, source_target_pairs={{28,0},{32,4},{36,8},{40,12},{44,16},{48,20},{52,24},{56,28},{60,3... | collective-permute-start | bytes 49160 | tf_op jit(solution)/shard_map/ppermute | solution.py:37
  309.9 30.2 %collective-permute-start.35 = (bf16[2,8,512]{2,1,0:T(8,128)(2,1)S(1)}, bf16[2,8,512]{2,1,0:T(8,128)(2,1)S(1)}, u32[]{:S(2)}, u32[]{:S(2)}) collective-permute-start(bf16[2,8,512]{2,1,0:T(8,128)(2,1)S(1)} %get-tuple-element.244), channel_id=1, source_target_pairs={{32,0},{36,4},{40,8},{44,12},{48,16},{52,20},{56,24},{60,28},{64,3... | collective-permute-start | bytes 49160 | tf_op jit(solution)/shard_map/ppermute | solution.py:37
  318.7 30.1 %collective-permute-start.28 = (bf16[2,32,512]{2,1,0:T(8,128)(2,1)S(1)}, bf16[2,32,512]{2,1,0:T(8,128)(2,1)S(1)}, u32[]{:S(2)}, u32[]{:S(2)}) collective-permute-start(bf16[2,32,512]{2,1,0:T(8,128)(2,1)S(1)} %get-tuple-element.249), channel_id=1, source_target_pairs={{12,0},{16,4},{20,8},{24,12},{28,16},{32,20},{36,24},{40,28},{44,3... | collective-permute-start | bytes 196616 | tf_op jit(solution)/shard_map/ppermute | solution.py:37
  322.1 20.9 %collective-permute-start.34 = (bf16[2,8,512]{2,1,0:T(8,128)(2,1)S(1)}, bf16[2,8,512]{2,1,0:T(8,128)(2,1)S(1)}, u32[]{:S(2)}, u32[]{:S(2)}) collective-permute-start(bf16[2,8,512]{2,1,0:T(8,128)(2,1)S(1)} %get-tuple-element.245), channel_id=1, source_target_pairs={{36,0},{40,4},{44,8},{48,12},{52,16},{56,20},{60,24},{64,28},{68,3... | collective-permute-start | bytes 49160 | tf_op jit(solution)/shard_map/ppermute | solution.py:37
  330.5 15.7 %collective-permute-start.33 = (bf16[2,8,512]{2,1,0:T(8,128)(2,1)S(1)}, bf16[2,8,512]{2,1,0:T(8,128)(2,1)S(1)}, u32[]{:S(2)}, u32[]{:S(2)}) collective-permute-start(bf16[2,8,512]{2,1,0:T(8,128)(2,1)S(1)} %slice_bitcast_fusion.24), channel_id=1, source_target_pairs={{40,0},{44,4},{48,8},{52,12},{56,16},{60,20},{64,24},{68,28},{72,3... | collective-permute-start | bytes 49160 | tf_op jit(solution)/shard_map/ppermute | solution.py:37
  338.0 18.5 %collective-permute-start.26 = (f32[2,128,512]{2,1,0:T(8,128)S(1)}, f32[2,128,512]{2,1,0:T(8,128)S(1)}, u32[]{:S(2)}, u32[]{:S(2)}) collective-permute-start(f32[2,128,512]{2,1,0:T(8,128)S(1)} %get-tuple-element.221), channel_id=1, source_target_pairs={{4,0},{8,4},{12,8},{16,12},{20,16},{24,20},{28,24},{32,28},{36,32}... | collective-permute-start | bytes 1572872 | tf_op jit(solution)/shard_map/ppermute | solution.py:37
  340.0 16.4 %collective-permute-start.27 = (f32[2,128,512]{2,1,0:T(8,128)S(1)}, f32[2,128,512]{2,1,0:T(8,128)S(1)}, u32[]{:S(2)}, u32[]{:S(2)}) collective-permute-start(f32[2,128,512]{2,1,0:T(8,128)S(1)} %get-tuple-element.222), channel_id=1, source_target_pairs={{0,4},{4,8},{8,12},{12,16},{16,20},{20,24},{24,28},{28,32},{32,36}... | collective-permute-start | bytes 1572872 | tf_op jit(solution)/shard_map/ppermute | solution.py:37
  (25 other events, 305.0 us)
where the time goes:
time: 361 us; the launch traced here: 358 us
  starting transfers between devices  213 us (59%)
  waiting for transfers between devices  82.1 us (23%)
  local copies, waits for them, and re-layouts  20 us (6%)
  blocking collectives  18.5 us (5%)
  matrix products  12.4 us (3%)
  other arithmetic  10 us (3%)
    ppermute x50, starting transfers between devices, passed_along(): return lax.ppermute(block, axis, route)  206 us
    ppermute x50, waiting for transfers between devices, passed_along(): return lax.ppermute(block, axis, route)  80.5 us
    psum x1, blocking collectives, body(): energy = lax.psum(jnp.sum(mixed * mixed, axis=1), 'head')  10.8 us
    psum x1, blocking collectives, body(): agreement = lax.psum(jnp.sum(incoming * normed, axis=1), 'head')  7.75 us
    dot_general x8, matrix products, across(): lax.dot_general(left, right, (((0,), (0,)), ((), ())), preferred_element_...  7.41 us
  transfers between devices with their start and end apart: 52, of which 22 were waited for; matrix products, arithmetic and copies ran while one was open for 4% of the time, Pallas kernels for 0%

commit v1 on v0

v1 whole, which is shorter than its diff:
```python
import math

import jax
import jax.numpy as jnp
from jax import lax
from jax.experimental import pallas as pl
from jax.experimental.pallas import tpu as pltpu
from jax.sharding import PartitionSpec as P

HEADS = 16
HEAD_DIM = 128
POOL1 = 4
POOL2 = 16
REACH1 = 3
REACH2 = 11
MATCHED_FRAME_ADD = 1.0
NORM_EPSILON = 1e-06

MESH = pl.DeviceIdType.MESH
F32 = jnp.float32
BF16 = jnp.bfloat16
LOG2E = math.log2(math.e)
MASKED = -1e30

ROWS = 128
HALF = 256
ONE = ROWS // POOL1
TWO = ROWS // POOL2
POOLED = 2 * (ONE + TWO)
NEAR = 3 * ROWS
FAR = 384

STEPS_ONE = (2, -1)


def direction(b):
    return 2 * b - 1


REL_ONE = [-2 * steps * direction(b) + b for b in (0, 1) for steps in STEPS_ONE] + [-1, 2]


def relative_two(side):
    sigma = direction(side)
    spots = [(2, 1 - side), (3, 1 - side), (3, side), (4, 1 - side), (4, side), (5, 1 - side), (5, side), (6, side)]
    return [-2 * k * sigma + b for k, b in spots]


REL_TWO = [relative_two(0), relative_two(1)]
REL_MIDDLE = REL_ONE + [REL_TWO[0][0], REL_TWO[1][0]]
REL_LAST = REL_TWO[0][1:] + REL_TWO[1][1:]
OWN, SIDE, MIDDLE, LAST = slice(0, 256), slice(256, 384), slice(384, 640), slice(640, 768)


def dot_nt(a, b):
    return lax.dot_general(a, b, (((1,), (1,)), ((), ())), preferred_element_type=F32)


def dot_tn(a, b):
    return lax.dot_general(a, b, (((0,), (0,)), ((), ())), preferred_element_type=F32)


def dot(a, b):
    return jnp.dot(a, b, preferred_element_type=F32)


def pool_matrix():
    r = lax.broadcasted_iota(jnp.int32, (ONE + TWO, ROWS), 0)
    t = lax.broadcasted_iota(jnp.int32, (ONE + TWO, ROWS), 1)
    one = jnp.where((t >> 2) == r, 1.0 / POOL1, 0.0)
    two = jnp.where((t >> 4) == r - ONE, 1.0 / POOL2, 0.0)
    return jnp.where(r < ONE, one, two).astype(BF16)


def spread_matrix():
    t = lax.broadcasted_iota(jnp.int32, (ROWS, ONE + TWO), 0)
    r = lax.broadcasted_iota(jnp.int32, (ROWS, ONE + TWO), 1)
    one = jnp.where((t >> 2) == r, 1.0 / POOL1, 0.0)
    two = jnp.where((t >> 4) == r - ONE, 1.0 / POOL2, 0.0)
    return jnp.where(r < ONE, one, two).astype(BF16)


def column_of(row):
    i = lax.broadcasted_iota(jnp.int32, (ROWS, ROWS), 0)
    j = lax.broadcasted_iota(jnp.int32, (ROWS, ROWS), 1)
    return jnp.sum(jnp.where(i == j, row, 0.0), axis=1, keepdims=True)


def row_of(column):
    i = lax.broadcasted_iota(jnp.int32, (ROWS, ROWS), 0)
    j = lax.broadcasted_iota(jnp.int32, (ROWS, ROWS), 1)
    return jnp.sum(jnp.where(i == j, column, 0.0), axis=0, keepdims=True)


def kernel(
    q_hbm, k_hbm, v_hbm, g_hbm, level_hbm, frame_hbm,
    att_hbm, dq_hbm, dk_hbm, dv_hbm,
    kv_own, q_two, g_two, kv_near, pooled, one_in, two_in, k_middle, v_middle, k_last, v_last,
    level_s, frame_v, near_bias, far_bias, weight, turned, mixed, stats,
    mixed_grad, att, dq, near_out, pool_out, two_out, sib_out, fold_out,
    pass_in, four_in, fold_in, near_back, one_back, two_back, sib_back, dk, dv,
    local_sem, send_sem, sib_recv, near_recv, one_recv, two_recv, stat_recv, pass_recv, fold_recv,
    back_near_recv, back_one_recv, back_two_recv, out_recv,
):
    blocks = lax.axis_size("seq")
    chips = blocks // 2
    heads = lax.axis_size("head")
    me = lax.axis_index("seq")
    lane = lax.axis_index("head")
    chip = me // 2
    core = me % 2
    other = 1 - core
    d = direction(core)

    def at(steps, c):
        return {"seq": ((chip + steps + chips) % chips) * 2 + c}

    sibling = {"seq": chip * 2 + other}

    def half(h):
        return pl.ds(pl.multiple_of(h * HALF, HALF), HALF)

    def remote(src, dst, send, recv, device):
        return pltpu.make_async_remote_copy(
            src_ref=src, dst_ref=dst, send_sem=send, recv_sem=recv, device_id=device, device_id_type=MESH
        )

    def inside(*steps, sided=()):
        away = [s for s in steps] + [s * d for s in sided]
        known = True
        for s in away:
            known = known & (chip + s >= 0) & (chip + s < chips)
        return (steps, sided), known

    def only(when, act):
        if when is None:
            act()
        else:
            pl.when(when[1])(act)

    sent = 0
    started = []

    def send(src, dst, recv, device, when=None):
        nonlocal sent
        copy = remote(src, dst, send_sem.at[sent], recv, device)
        sent += 1
        only(when, copy.start)
        started.append((copy, when))

    def flush():
        groups = {}
        for copy, when in started:
            groups.setdefault(when and when[0], (when, []))[1].append(copy)
        started.clear()
        for when, copies in groups.values():

            def wait_all(copies=copies):
                for copy in copies:
                    copy.wait_send()

            only(when, wait_all)

    def arrived(ref, sem, when=None):
        only(when, remote(ref, ref, sem, sem, sibling).wait_recv)

    @pl.when((chip < 6) | (chip >= chips - 6))
    def _():
        for ref in (one_in, two_in, pass_in, four_in, fold_in, near_back, one_back, two_back):
            ref[...] = jnp.zeros(ref.shape, ref.dtype)
        for s in (0, 3):
            kv_near[s] = jnp.zeros(kv_near.shape[1:], BF16)

    mine = pl.ds(pl.multiple_of(core * ROWS, ROWS), ROWS)
    theirs = pl.ds(pl.multiple_of(other * ROWS, ROWS), ROWS)
    k_rows, v_rows = pl.ds(0, ROWS), pl.ds(ROWS, ROWS)
    locals_in = [
        pltpu.make_async_copy(k_hbm, kv_own.at[k_rows], local_sem.at[0]),
        pltpu.make_async_copy(v_hbm, kv_own.at[v_rows], local_sem.at[1]),
        pltpu.make_async_copy(level_hbm, level_s, local_sem.at[2]),
        pltpu.make_async_copy(frame_hbm, frame_v, local_sem.at[3]),
        pltpu.make_async_copy(k_hbm.at[:, half(core)], kv_near.at[1 + core, k_rows], local_sem.at[4]),
        pltpu.make_async_copy(v_hbm.at[:, half(core)], kv_near.at[1 + core, v_rows], local_sem.at[5]),
        pltpu.make_async_copy(q_hbm.at[:, half(core)], q_two.at[mine], local_sem.at[6]),
        pltpu.make_async_copy(g_hbm.at[:, half(core)], g_two.at[mine], local_sem.at[7]),
    ]
    for copy in locals_in[:2]:
        copy.start()

    barrier = pltpu.get_barrier_semaphore()
    partners = [sibling]
    for k in range(1, heads):
        for c in (0, 1):
            partners.append({"seq": chip * 2 + c, "head": (lane + k) % heads})
    expected = len(partners)

    def greet(devices):
        for device in devices:
            pl.semaphore_signal(barrier, inc=1, device_id=device, device_id_type=MESH)

    for steps in (2, -2, 1, -1):
        when = inside(steps)
        only(when, lambda: greet([at(steps, 0), at(steps, 1)]))
        expected = expected + jnp.where(when[1], 2, 0)
    greet(partners)
    for copy in locals_in[2:]:
        copy.start()

    locals_in[0].wait()
    locals_in[1].wait()
    pool = pool_matrix()
    k_pool = dot(pool, kv_own[:ROWS])
    v_pool = dot(pool, kv_own[ROWS:])
    pooled[0 : 2 * ONE, :] = jnp.concatenate([k_pool[:ONE], v_pool[:ONE]], axis=0).astype(BF16)
    pooled[2 * ONE :, :] = jnp.concatenate([k_pool[ONE:], v_pool[ONE:]], axis=0).astype(BF16)

    pl.semaphore_wait(barrier, expected)

    def send_two(steps, side, spot):
        for h in (0, 1):
            send(
                pooled.at[pl.ds(2 * ONE, 2 * TWO), half(h)], two_in.at[side, spot],
                two_recv.at[side, spot], at(steps * d, h), inside(sided=(steps,)),
            )

    send_two(2, core, 1)
    send_two(-2, other, 0)
    for h in (0, 1):
        send(
            pooled.at[:, half(h)], one_in.at[core * 2 + 1],
            one_recv.at[core * 2 + 1], at(-d, h), inside(sided=(-1,)),
        )
    send(kv_own.at[:, half(other)], kv_near.at[1 + core], sib_recv.at[0], sibling)
    send(q_hbm.at[:, half(other)], q_two.at[mine], sib_recv.at[2], sibling)
    for h in (0, 1):
        send(kv_own.at[:, half(h)], kv_near.at[3 - 3 * core], near_recv.at[core], at(d, h), inside(sided=(1,)))
    send(g_hbm.at[:, half(other)], g_two.at[mine], sib_recv.at[3], sibling)

    locals_in[2].wait()
    locals_in[3].wait()
    table = [level_s[0, i] for i in range(4)]
    spot = lax.broadcasted_iota(jnp.int32, (8, FAR), 1)
    row = jnp.full((8, FAR), MASKED, F32)

    def level_at(offset):
        choice = jnp.where(offset == -3, table[0], table[1])
        choice = jnp.where(offset == 2, table[2], choice)
        return jnp.where(offset == 3, table[3], choice)

    def slot_bias(rel, wanted, most, bias):
        offset = rel - core
        distance = jnp.abs(offset)
        block = 2 * chip + rel
        inside = (distance >= 2) & (distance <= most) & (block >= 0) & (block < blocks)
        chosen = (distance > REACH1) | (level_at(offset) == wanted)
        return jnp.where(inside & chosen, bias * LOG2E, MASKED)

    for s, rel in enumerate(REL_ONE):
        value = slot_bias(rel, 1, REACH1, math.log(POOL1))
        row = jnp.where((spot >= s * ONE) & (spot < (s + 1) * ONE), value, row)
    for s, rel in enumerate(REL_MIDDLE + REL_LAST):
        low = len(REL_ONE) * ONE + s * TWO
        value = slot_bias(rel, 2, REACH2, math.log(POOL2))
        row = jnp.where((spot >= low) & (spot < low + TWO), value, row)
    far_bias[core] = row
    send(far_bias.at[core], far_bias.at[core], sib_recv.at[4], sibling)

    lengths = frame_v[...].astype(F32)
    count = lengths.shape[1]
    i = lax.broadcasted_iota(jnp.int32, (count, count), 0)
    j = lax.broadcasted_iota(jnp.int32, (count, count), 1)
    ends_column = jnp.sum(jnp.where(j <= i, lengths, 0.0), axis=1, keepdims=True)
    ends_row = jnp.sum(jnp.where(i == j, ends_column, 0.0), axis=0, keepdims=True)
    start = (2 * chip - 1) * ROWS
    key_place = start + lax.broadcasted_iota(jnp.int32, (1, 4 * ROWS), 1)
    key_frame = jnp.sum(jnp.where(key_place.astype(F32) >= ends_column, 1.0, 0.0), axis=0, keepdims=True)
    key_inside = (key_place >= 0) & (key_place < blocks * ROWS)
    for b in (0, 1):
        place = start + (b + 1) * ROWS + lax.broadcasted_iota(jnp.int32, (ROWS, 1), 0)
        frame = jnp.sum(jnp.where(place.astype(F32) >= ends_row, 1.0, 0.0), axis=1, keepdims=True)
        matched = jnp.where(frame == key_frame, MATCHED_FRAME_ADD * LOG2E, 0.0)
        matched = jnp.where(key_inside, matched, MASKED)
        rows = slice(b * ROWS, (b + 1) * ROWS)
        near_bias[rows, OWN] = matched[:, ROWS : 3 * ROWS]
        near_bias[rows, SIDE] = matched[:, 3 * b * ROWS : (3 * b + 1) * ROWS]

    scale = LOG2E / math.sqrt(HEAD_DIM)
    columns = [slice(h * HEAD_DIM, (h + 1) * HEAD_DIM) for h in (0, 1)]
    first, second = slice(0, ROWS), slice(ROWS, 2 * ROWS)
    highs, totals, accs = [[], []], [None, None], [None, None]

    def far_of(part):
        low, high = part.start - MIDDLE.start, part.stop - MIDDLE.start
        shape = (ROWS, high - low)
        return jnp.concatenate([jnp.broadcast_to(far_bias[b, 0:1, low:high], shape) for b in (0, 1)], axis=0)

    def attend(h, part, scores, product):
        top = jnp.max(scores, axis=1, keepdims=True)
        if highs[h]:
            top = jnp.maximum(highs[h][-1], top)
        e = jnp.exp2(scores - top)
        weight[h, :, part] = e
        total = jnp.sum(e, axis=1, keepdims=True)
        acc = product(e.astype(BF16))
        if highs[h]:
            alpha = jnp.exp2(highs[h][-1] - top)
            total = totals[h] * alpha + total
            acc = accs[h] * alpha + acc
        highs[h].append(top)
        totals[h], accs[h] = total, acc

    rows_of = (first, second)

    def own_of(kind, h):
        return kv_near[1:3, rows_of[kind], columns[h]].reshape(2 * ROWS, HEAD_DIM)

    for side in (0, 1):
        sigma = direction(side)
        pair, two = pl.ds(0, 2), -2 * sigma
        for s in (0, 1):
            arrived(two_in.at[side, s], two_recv.at[side, s], inside(two))
        send(
            two_in.at[side, pair], two_in.at[side, pl.ds(4, 2)],
            two_recv.at[side, 4], at(2 * sigma, core), inside(two, 2 * sigma),
        )
        send(
            two_in.at[side, pair], two_in.at[side, pl.ds(2, 2)],
            two_recv.at[side, 2], at(sigma, core), inside(two, sigma),
        )

    locals_in[4].wait()
    locals_in[6].wait()
    locals_in[5].wait()
    arrived(kv_near.at[1 + other], sib_recv.at[0])
    arrived(q_two.at[theirs], sib_recv.at[2])
    for h in (0, 1):
        scores = dot_nt(q_two[:, columns[h]], own_of(0, h)) * scale + near_bias[:, OWN]
        attend(h, OWN, scores, lambda e: dot(e, own_of(1, h)))

    for side in (0, 1):
        sigma = direction(side)
        pair, four = pl.ds(4, 2), -4 * sigma
        arrived(two_in.at[side, pair], two_recv.at[side, 4], inside(four))
        send(
            two_in.at[side, pair], two_in.at[side, pl.ds(6, 2)],
            two_recv.at[side, 6], at(sigma, core), inside(four, sigma),
        )
        send(two_in.at[side, 5], two_in.at[side, 8], two_recv.at[side, 8], at(2 * sigma, core), inside(four, 2 * sigma))

    arrived(kv_near.at[3], near_recv.at[0], inside(1))
    arrived(kv_near.at[0], near_recv.at[1], inside(-1))
    near_pools = [(dot(pool, kv_near[s, first]), dot(pool, kv_near[s, second])) for s in (0, 3)]
    ones_only = pl.ds(0, 2 * ONE)
    for i, side in ((0, 1), (1, 0)):
        sigma = direction(side)
        fold_out[i] = jnp.concatenate([p[:ONE] for p in near_pools[i]], axis=0).astype(BF16)
        send(
            fold_out.at[i], one_in.at[side * 2, ones_only],
            one_recv.at[side * 2], at(sigma, core), inside(-sigma, sigma),
        )
    for h in (0, 1):
        query = q_two[:, columns[h]]
        scores = jnp.concatenate(
            [dot_nt(query[first], kv_near[0, first, columns[h]]), dot_nt(query[second], kv_near[3, first, columns[h]])], axis=0
        )
        attend(
            h, SIDE, scores * scale + near_bias[:, SIDE],
            lambda e: jnp.concatenate(
                [dot(e[first], kv_near[0, second, columns[h]]), dot(e[second], kv_near[3, second, columns[h]])], axis=0
            ),
        )

    for side in (0, 1):
        sigma = direction(side)
        arrived(one_in.at[side * 2, ones_only], one_recv.at[side * 2], inside(-2 * sigma))
        arrived(one_in.at[side * 2 + 1], one_recv.at[side * 2 + 1], inside(sigma))
    arrived(far_bias.at[other], sib_recv.at[4])
    nearest = [two_in[0, 1], one_in[1, 2 * ONE :], two_in[1, 1], one_in[3, 2 * ONE :]]
    nearest = [x.astype(F32) for x in nearest]
    for kind, middle in ((0, k_middle), (1, v_middle)):
        ones = slice(kind * ONE, (kind + 1) * ONE)
        rows = slice(kind * TWO, (kind + 1) * TWO)
        for s in range(4):
            middle[s * ONE : (s + 1) * ONE] = one_in[s, ones]
        for i in (0, 1):
            middle[(4 + i) * ONE : (5 + i) * ONE] = fold_out[i, ones]
        parts = [x[rows] for x in nearest] + [p[kind][ONE:] for p in near_pools]
        parts += [two_in[side, 0].astype(F32)[rows] for side in (0, 1)]
        middle[6 * ONE :] = jnp.concatenate(parts, axis=0).astype(BF16)
    for h in (0, 1):
        scores = dot_nt(q_two[:, columns[h]], k_middle[:, columns[h]]) * scale + far_of(MIDDLE)
        attend(h, MIDDLE, scores, lambda e: dot(e, v_middle[:, columns[h]]))

    for side in (0, 1):
        sigma = direction(side)
        for s, steps in ((2, 3), (6, 5)):
            arrived(two_in.at[side, pl.ds(s, 2)], two_recv.at[side, s], inside(-steps * sigma))
        arrived(two_in.at[side, 8], two_recv.at[side, 8], inside(-6 * sigma))
    twos = [two_in[side, 2:].astype(F32) for side in (0, 1)]
    for kind, last in ((0, k_last), (1, v_last)):
        rows = slice(kind * TWO, (kind + 1) * TWO)
        parts = [t[:, rows].reshape(7 * TWO, HALF) for t in twos] + [jnp.zeros((2 * TWO, HALF), F32)]
        last[...] = jnp.concatenate(parts, axis=0).astype(BF16)
    for h in (0, 1):
        scores = dot_nt(q_two[:, columns[h]], k_last[:, columns[h]]) * scale + far_of(LAST)
        attend(h, LAST, scores, lambda e: dot(e, v_last[:, columns[h]]))
    inverse_totals = [1.0 / totals[h] for h in (0, 1)]
    for h in (0, 1):
        mixed[:, columns[h]] = accs[h] * inverse_totals[h]

    locals_in[7].wait()
    arrived(g_two.at[theirs], sib_recv.at[3])
    mates = 2 * heads
    place = lane * 2 + core
    value = mixed[...]
    energy = jnp.sum(value * value, axis=1, keepdims=True)
    product = jnp.sum(value * g_two[...].astype(F32), axis=1, keepdims=True)
    stats[place] = jnp.concatenate(
        [row_of(energy[:ROWS]), row_of(energy[ROWS:]), row_of(product[:ROWS]), row_of(product[ROWS:]), jnp.zeros((4, ROWS), F32)],
        axis=0,
    )
    for k in range(1, mates):
        to = (place + k) % mates
        send(stats.at[place], stats.at[place], stat_recv.at[place], {"seq": chip * 2 + to % 2, "head": to // 2})
    for h in (0, 1):
        for index, part in enumerate((OWN, SIDE, MIDDLE, LAST)):
            weights = weight[h, :, part] * (jnp.exp2(highs[h][index] - highs[h][-1]) * inverse_totals[h])
            weight[h, :, part] = weights
            turned[h, part, :] = weights.T.astype(BF16)
    for k in range(1, mates):
        source = (place + k) % mates
        arrived(stats.at[source], stat_recv.at[source])
    summed = stats[0]
    for k in range(1, mates):
        summed = summed + stats[k]
    width = HEADS * HEAD_DIM
    deltas = [[], []]
    for b, rows in ((0, first), (1, second)):
        inverse = lax.rsqrt(column_of(summed[b : b + 1]) / width + NORM_EPSILON)
        agreement = column_of(summed[2 + b : 3 + b]) * inverse
        normed = mixed[rows] * inverse
        att[rows] = normed.astype(BF16)
        grad = (inverse * (g_two[rows].astype(F32) - normed * (agreement / width))).astype(BF16)
        mixed_grad[rows] = grad
        both = grad.astype(F32) * mixed[rows]
        for h in (0, 1):
            deltas[h].append(jnp.sum(both[:, columns[h]], axis=1, keepdims=True))
    deltas = [jnp.concatenate(deltas[h], axis=0) for h in (0, 1)]

    unscale = 1.0 / math.sqrt(HEAD_DIM)
    query_grads = [None, None]

    def slopes_of(h, part, products):
        weights = weight[h, :, part]
        return (weights * (products - deltas[h])).astype(BF16)

    def plain_backward(part, k_ref, v_ref):
        k_parts, v_parts = [], []
        for h in (0, 1):
            grad = mixed_grad[:, columns[h]]
            slopes = slopes_of(h, part, dot_nt(grad, v_ref(h)))
            change = dot(slopes, k_ref(h))
            query_grads[h] = change if query_grads[h] is None else query_grads[h] + change
            k_parts.append(dot_tn(slopes, q_two[:, columns[h]]) * unscale)
            v_parts.append(dot(turned[h, part, :], grad))
        return jnp.concatenate(k_parts, axis=1), jnp.concatenate(v_parts, axis=1)

    def two_rows(pair, low):
        return jnp.concatenate([g[low : low + TWO] for g in pair], axis=0)

    last = plain_backward(LAST, lambda h: k_last[:, columns[h]], lambda h: v_last[:, columns[h]])
    for side in (0, 1):
        sigma = direction(side)
        for s in (1, 2, 5, 6, 7):
            two_out[side, s] = two_rows(last, (side * 7 + s - 1) * TWO).astype(BF16)
        send(
            two_out.at[side, pl.ds(5, 2)], pass_in.at[side, pl.ds(0, 2)],
            pass_recv.at[side, 0], at(-sigma, core), inside(-5 * sigma),
        )
        send(two_out.at[side, 7], pass_in.at[side, 4], pass_recv.at[side, 2], at(-2 * sigma, core), inside(-6 * sigma))
        send(
            two_out.at[side, pl.ds(1, 2)], pass_in.at[side, pl.ds(2, 2)],
            pass_recv.at[side, 1], at(-sigma, core), inside(-3 * sigma),
        )
    out_att = pltpu.make_async_copy(att.at[mine], att_hbm.at[:, half(core)], local_sem.at[8])
    out_att.start()
    send(att.at[theirs], att_hbm.at[:, half(core)], out_recv.at[0], sibling)

    middle = plain_backward(MIDDLE, lambda h: k_middle[:, columns[h]], lambda h: v_middle[:, columns[h]])
    for s in range(4):
        for kind in (0, 1):
            pool_out[s, kind * ONE : (kind + 1) * ONE] = middle[kind][s * ONE : (s + 1) * ONE].astype(BF16)
    for b in (0, 1):
        s = 2 * b + 1
        pool_out[s, 2 * ONE :] = two_rows(middle, 6 * ONE + s * TWO).astype(BF16)
        send(pool_out.at[s], one_back.at[core], back_one_recv.at[core], at(direction(b), b), inside(direction(b)))
    for side in (0, 1):
        sigma = direction(side)
        send(
            pool_out.at[2 * side, ones_only], fold_in.at[side],
            fold_recv.at[side], at(-sigma, core), inside(-2 * sigma),
        )

    spread = spread_matrix()
    k_sides, v_sides = [[], []], [[], []]
    for h in (0, 1):
        grad = mixed_grad[:, columns[h]]
        query = q_two[:, columns[h]]
        products = jnp.concatenate(
            [dot_nt(grad[first], kv_near[0, second, columns[h]]), dot_nt(grad[second], kv_near[3, second, columns[h]])], axis=0
        )
        slopes = slopes_of(h, SIDE, products)
        query_grads[h] = query_grads[h] + jnp.concatenate(
            [dot(slopes[first], kv_near[0, first, columns[h]]), dot(slopes[second], kv_near[3, first, columns[h]])], axis=0
        )
        for b, rows in ((0, second), (1, first)):
            k_sides[b].append(dot_tn(slopes[rows], query[rows]) * unscale)
            v_sides[b].append(dot(turned[h, SIDE, rows], grad[rows]))
    for side in (0, 1):
        sigma = direction(side)
        four = -4 * sigma
        arrived(pass_in.at[side, pl.ds(0, 2)], pass_recv.at[side, 0], inside(sigma, four))
        arrived(pass_in.at[side, 4], pass_recv.at[side, 2], inside(2 * sigma, four))
        passed = [pass_in[side, s].astype(F32) for s in (0, 1, 4)]
        two_out[side, 3] = (two_rows(last, (side * 7 + 2) * TWO) + passed[0]).astype(BF16)
        two_out[side, 4] = (two_rows(last, (side * 7 + 3) * TWO) + passed[1] + passed[2]).astype(BF16)
        send(two_out.at[side, pl.ds(3, 2)], four_in.at[side], pass_recv.at[side, 3], at(-2 * sigma, core), inside(four))

    for b in (0, 1):
        p = 5 - b
        sigma = direction(b)
        arrived(fold_in.at[b], fold_recv.at[b], inside(sigma, -sigma))
        folded = fold_in[b].astype(F32)
        for kind, sides in ((0, k_sides), (1, v_sides)):
            pools = middle[kind]
            small = jnp.concatenate(
                [pools[p * ONE : (p + 1) * ONE] + folded[kind * ONE : (kind + 1) * ONE], pools[6 * ONE + p * TWO : 6 * ONE + (p + 1) * TWO]], axis=0
            )
            near_out[b, kind * ROWS : (kind + 1) * ROWS] = (
                jnp.concatenate(sides[b], axis=1) + dot(spread, small.astype(BF16))
            ).astype(BF16)
        send(near_out.at[b], near_back.at[core], back_near_recv.at[core], at(-direction(b), b), inside(-direction(b)))

    own = plain_backward(OWN, lambda h: own_of(0, h), lambda h: own_of(1, h))
    for kind in (0, 1):
        sib_out[kind * ROWS : (kind + 1) * ROWS] = jnp.where(core == 0, own[kind][second], own[kind][first]).astype(BF16)
    send(sib_out, sib_back, out_recv.at[1], sibling)
    for h in (0, 1):
        dq[:, columns[h]] = (query_grads[h] * unscale).astype(BF16)
    out_dq = pltpu.make_async_copy(dq.at[mine], dq_hbm.at[:, half(core)], local_sem.at[9])
    out_dq.start()
    send(dq.at[theirs], dq_hbm.at[:, half(core)], out_recv.at[2], sibling)

    for side in (0, 1):
        sigma = direction(side)
        two = -2 * sigma
        arrived(pass_in.at[side, pl.ds(2, 2)], pass_recv.at[side, 1], inside(sigma, two))
        arrived(four_in.at[side], pass_recv.at[side, 3], inside(2 * sigma, two))
        passed = pass_in[side, 2:4].astype(F32) + four_in[side].astype(F32)
        two_out[side, 0] = (two_rows(middle, 6 * ONE + (6 + side) * TWO) + passed[0]).astype(BF16)
        two_out[side, 8] = (two_rows(middle, 6 * ONE + 2 * side * TWO) + passed[1]).astype(BF16)
        send(two_out.at[side, 0], two_back.at[core, 0], back_two_recv.at[core, 0], at(two, 1 - side), inside(two))
        send(two_out.at[side, 8], two_back.at[core, 1], back_two_recv.at[core, 1], at(two, side), inside(two))

    arrived(sib_back, out_recv.at[1])
    mine_grads = [jnp.where(core == 0, own[kind][first], own[kind][second]) for kind in (0, 1)]
    bases = {}
    for h in (0, 1):
        arrived(one_back.at[h], back_one_recv.at[h], inside(sided=(-1,)))
        for j, steps in enumerate((-2, 2)):
            arrived(two_back.at[h, j], back_two_recv.at[h, j], inside(sided=(steps,)))
        ones = one_back[h].astype(F32)
        twos = ones[2 * ONE :] + two_back[h, 0].astype(F32) + two_back[h, 1].astype(F32)
        for kind in (0, 1):
            rows = slice(kind * ROWS, (kind + 1) * ROWS)
            small = jnp.concatenate([ones[kind * ONE : (kind + 1) * ONE], twos[kind * TWO : (kind + 1) * TWO]], axis=0)
            grads = jnp.where(core == h, mine_grads[kind], sib_back[rows].astype(F32))
            bases[h, kind] = grads + dot(spread, small.astype(BF16))
    arrived(att_hbm.at[:, half(other)], out_recv.at[0])
    arrived(dq_hbm.at[:, half(other)], out_recv.at[2])
    flush()
    for h in (0, 1):
        arrived(near_back.at[h], back_near_recv.at[h], inside(sided=(1,)))
    outs = [out_att, out_dq]
    for kind, out, out_hbm in ((0, dk, dk_hbm), (1, dv, dv_hbm)):
        rows = slice(kind * ROWS, (kind + 1) * ROWS)
        for h in (0, 1):
            out[:, h * HALF : (h + 1) * HALF] = (bases[h, kind] + near_back[h, rows].astype(F32)).astype(BF16)
        outs.append(pltpu.make_async_copy(out, out_hbm, local_sem.at[10 + kind]))
        outs[-1].start()
    for copy in outs:
        copy.wait()


def write_out(*refs):
    *arrays, sems = refs
    copies = [pltpu.make_async_copy(arrays[i], arrays[4 + i], sems.at[i]) for i in range(4)]
    for copy in copies:
        copy.start()
    for copy in copies:
        copy.wait()


def body(queries, keys, values, out_grad, level_choice, frame_lengths):
    rows, width = queries.shape
    vmem = pltpu.VMEM
    dma = pltpu.SemaphoreType.DMA
    out = jax.ShapeDtypeStruct((rows, width), BF16)
    limit = 40 * 1024 * 1024
    arrays = (queries, keys, values, out_grad, level_choice, frame_lengths.reshape(1, -1))
    results = pl.pallas_call(
        kernel,
        out_shape=(out, out, out, out),
        in_specs=[pl.BlockSpec(memory_space=pl.ANY)] * 6,
        out_specs=(pl.BlockSpec(memory_space=pl.ANY),) * 4,
        scratch_shapes=[
            vmem((2 * ROWS, width), BF16),
            vmem((2 * ROWS, HALF), BF16),
            vmem((2 * ROWS, HALF), BF16),
            vmem((4, 2 * ROWS, HALF), BF16),
            vmem((POOLED, width), BF16),
            vmem((4, POOLED, HALF), BF16),
            vmem((2, 9, 2 * TWO, HALF), BF16),
            vmem((256, HALF), BF16),
            vmem((256, HALF), BF16),
            vmem((128, HALF), BF16),
            vmem((128, HALF), BF16),
            pltpu.SMEM((1, 4), jnp.int32),
            vmem((1, 64), jnp.int32),
            vmem((2 * ROWS, 384), F32),
            vmem((2, 8, FAR), F32),
            vmem((2, 2 * ROWS, 768), F32),
            vmem((2, 768, 2 * ROWS), BF16),
            vmem((2 * ROWS, HALF), F32),
            vmem((8, 8, ROWS), F32),
            vmem((2 * ROWS, HALF), BF16),
            vmem((2 * ROWS, HALF), BF16),
            vmem((2 * ROWS, HALF), BF16),
            vmem((2, 2 * ROWS, HALF), BF16),
            vmem((4, POOLED, HALF), BF16),
            vmem((2, 9, 2 * TWO, HALF), BF16),
            vmem((2 * ROWS, HALF), BF16),
            vmem((2, 2 * ONE, HALF), BF16),
            vmem((2, 5, 2 * TWO, HALF), BF16),
            vmem((2, 2, 2 * TWO, HALF), BF16),
            vmem((2, 2 * ONE, HALF), BF16),
            vmem((2, 2 * ROWS, HALF), BF16),
            vmem((2, POOLED, HALF), BF16),
            vmem((2, 2, 2 * TWO, HALF), BF16),
            vmem((2 * ROWS, HALF), BF16),
            vmem((ROWS, width), BF16),
            vmem((ROWS, width), BF16),
            dma((12,)),
            dma((64,)),
            dma((5,)),
            dma((2,)),
            dma((4,)),
            dma((2, 9)),
            dma((8,)),
            dma((2, 4)),
            dma((2,)),
            dma((2,)),
            dma((2,)),
            dma((2, 2)),
            dma((3,)),
        ],
        compiler_params=pltpu.CompilerParams(collective_id=0, has_side_effects=True, vmem_limit_bytes=limit),
        cost_estimate=pl.CostEstimate(flops=700_000_000, bytes_accessed=1_100_000, transcendentals=400_000),
    )(*[pltpu.with_memory_space_constraint(array, pltpu.HBM) for array in arrays])
    return pl.pallas_call(
        write_out,
        out_shape=(out, out, out, out),
        in_specs=[pl.BlockSpec(memory_space=pl.ANY)] * 4,
        out_specs=(pl.BlockSpec(memory_space=pl.ANY),) * 4,
        scratch_shapes=[dma((4,))],
        compiler_params=pltpu.CompilerParams(vmem_limit_bytes=limit),
        cost_estimate=pl.CostEstimate(flops=0, bytes_accessed=1_100_000, transcendentals=0),
    )(*results)


def solution(mesh):
    in_specs = (
        P("seq", "head"),
        P("seq", "head"),
        P("seq", "head"),
        P("seq", "head"),
        P("seq", None),
        P(),
    )
    out_specs = (P("seq", "head"), P("seq", "head"), P("seq", "head"), P("seq", "head"))
    return jax.shard_map(body, mesh=mesh, in_specs=in_specs, out_specs=out_specs, check_vma=False)
```

time: 361 us -> 45.4 us (0.13)
  starting transfers between devices: 213 us -> 0 us
  waiting for transfers between devices: 82.1 us -> 0 us
  Pallas kernels: 0 us -> 44.7 us
  local copies, waits for them, and re-layouts: 20 us -> 0 us
  blocking collectives: 18.5 us -> 0 us
  matrix products: 12.4 us -> 0 us
  other arithmetic: 10 us -> 0 us
    ppermute x52 -> x0, starting transfers between devices: 213 us -> none  [the longest x50 206 us: passed_along(): return lax.ppermute(block, axis, route)]
    ppermute x52 -> x0, waiting for transfers between devices: 82.1 us -> none  [the longest x50 80.5 us: passed_along(): return lax.ppermute(block, axis, route)]
    pallas_call x0 -> x2, Pallas kernels: none -> 44.7 us  [the longest x1 43.8 us: body(): pl.pallas_call(kernel, out_shape=(out, out, out, out), in_specs=[pl.Block...]
    psum x2 -> x0, blocking collectives: 18.5 us -> none  [the longest x1 10.8 us: body(): energy = lax.psum(jnp.sum(mixed * mixed, axis=1), 'head')]
    dot_general x28 -> x0, matrix products: 12.4 us -> none  [the longest x8 7.41 us: across(): lax.dot_general(left, right, (((0,), (0,)), ((), ())), preferred_element_...]
    another operation x11 -> x0, local copies, waits for them, and re-layouts: 5.36 us -> none  [the longest x3 2.3 us: body(): set_grads = jnp.stack([from_heads(key_set), from_heads(value_set)])]
    transpose x2 -> x0, local copies, waits for them, and re-layouts: 4.45 us -> none  [from_heads(): return array.transpose(1, 0, 2).reshape(array.shape[1], -1)]
    select_n x3 -> x0, other arithmetic: 4.06 us -> none  [the longest x1 3.28 us: body(): jnp.where(usable_two, math.log(POOL2), -jnp.inf).astype(jnp.float32)]
  transfers between devices with their start and end apart: 52 -> 0, of which waited for: 22 -> 0; matrix products, arithmetic and copies ran while one was open for 4% -> 0% of each run, Pallas kernels for 0% -> 0%
where the time goes in v1:
time: 45.4 us; the launch traced here: 45.3 us
  Pallas kernels  44.7 us (98%)
  between operations  0.64 us (1%)
    pallas_call x1, Pallas kernels, body(): pl.pallas_call(kernel, out_shape=(out, out, out, out), in_specs=[pl.Block...  43.8 us

profile of v1, /device:TPU:6, one launch (start us, length us, event | category | flops | bytes accessed | tf_op | source)
XLA Modules:
  0.0 45.3 jit_solution(15944502233421594572)
XLA Ops:
  0.6 43.8 %shard_map.93 = (bf16[128,512]{1,0:T(8,128)(2,1)S(1)}, bf16[128,512]{1,0:T(8,128)(2,1)S(1)}, bf16[128,512]{1,0:T(8,128)(2,1)S(1)}, bf16[128,512]{1,0:T(8,128)(2,1)S(1)}) custom-call(bf16[128,512]{1,0:T(8,128)(2,1)} %q_hbm.1, bf16[128,512]{1,0:T(8,128)(2,1)} %k_hbm.1, bf16[128,512]{1,0:T(8,128)(2,1)} %v_hbm.1, bf16[128,512]{1,0:T(8,128)(2,1)} %g_hbm.1, ...), custom_call_target="tpu_custom_call" | custom-call | flops 700000000 | bytes 1100000 | tf_op jit(solution)/shard_map/pallas_call | solution.py:611
  44.5 0.8 %shard_map.94 = (bf16[128,512]{1,0:T(8,128)(2,1)}, bf16[128,512]{1,0:T(8,128)(2,1)}, bf16[128,512]{1,0:T(8,128)(2,1)}, bf16[128,512]{1,0:T(8,128)(2,1)}) custom-call(bf16[128,512]{1,0:T(8,128)(2,1)S(1)} %get-tuple-element.8.refs_0_, bf16[128,512]{1,0:T(8,128)(2,1)S(1)} %get-tuple-element.9.refs_1_, bf16[128,512]{1,0:T(8,128)(2,1)S(1)} %get-tuple-element.10.refs_2_, ...), custom_call_target="tpu_custom_call" | custom-call | bytes 1100000 | tf_op jit(solution)/shard_map/pallas_call | solution.py:670

commit v2 on v1

--- a/solution.py
+++ b/solution.py
@@ -301,7 +301,10 @@
         e = jnp.exp2(scores - top)
         weight[h, :, part] = e
         total = jnp.sum(e, axis=1, keepdims=True)
-        acc = product(e.astype(BF16))
+        rounded = e.astype(BF16)
+        acc = product(rounded)
+        if part in (OWN, SIDE):
+            turned[h, part, :] = rounded.T
         if highs[h]:
             alpha = jnp.exp2(highs[h][-1] - top)
             total = totals[h] * alpha + total
@@ -422,11 +425,12 @@
     for k in range(1, mates):
         to = (place + k) % mates
         send(stats.at[place], stats.at[place], stat_recv.at[place], {"seq": chip * 2 + to % 2, "head": to // 2})
+    factors = [[], []]
     for h in (0, 1):
         for index, part in enumerate((OWN, SIDE, MIDDLE, LAST)):
-            weights = weight[h, :, part] * (jnp.exp2(highs[h][index] - highs[h][-1]) * inverse_totals[h])
-            weight[h, :, part] = weights
-            turned[h, part, :] = weights.T.astype(BF16)
+            factors[h].append(jnp.exp2(highs[h][index] - highs[h][-1]) * inverse_totals[h])
+            if part in (MIDDLE, LAST):
+                turned[h, part, :] = weight[h, :, part].astype(BF16).T
     for k in range(1, mates):
         source = (place + k) % mates
         arrived(stats.at[source], stat_recv.at[source])
@@ -440,9 +444,9 @@
         agreement = column_of(summed[2 + b : 3 + b]) * inverse
         normed = mixed[rows] * inverse
         att[rows] = normed.astype(BF16)
-        grad = (inverse * (g_two[rows].astype(F32) - normed * (agreement / width))).astype(BF16)
+        grad = inverse * (g_two[rows].astype(F32) - normed * (agreement / width))
         mixed_grad[rows] = grad
-        both = grad.astype(F32) * mixed[rows]
+        both = grad.astype(BF16).astype(F32) * mixed[rows]
         for h in (0, 1):
             deltas[h].append(jnp.sum(both[:, columns[h]], axis=1, keepdims=True))
     deltas = [jnp.concatenate(deltas[h], axis=0) for h in (0, 1)]
@@ -450,15 +454,18 @@
     unscale = 1.0 / math.sqrt(HEAD_DIM)
     query_grads = [None, None]
 
-    def slopes_of(h, part, products):
-        weights = weight[h, :, part]
-        return (weights * (products - deltas[h])).astype(BF16)
+    def scaled(h, part):
+        factor = factors[h][(OWN, SIDE, MIDDLE, LAST).index(part)]
+        return (mixed_grad[:, columns[h]] * factor).astype(BF16), deltas[h] * factor
+
+    def slopes_of(h, part, products, delta):
+        return (weight[h, :, part] * (products - delta)).astype(BF16)
 
     def plain_backward(part, k_ref, v_ref):
         k_parts, v_parts = [], []
         for h in (0, 1):
-            grad = mixed_grad[:, columns[h]]
-            slopes = slopes_of(h, part, dot_nt(grad, v_ref(h)))
+            grad, delta = scaled(h, part)
+            slopes = slopes_of(h, part, dot_nt(grad, v_ref(h)), delta)
             change = dot(slopes, k_ref(h))
             query_grads[h] = change if query_grads[h] is None else query_grads[h] + change
             k_parts.append(dot_tn(slopes, q_two[:, columns[h]]) * unscale)
@@ -504,12 +511,12 @@
     spread = spread_matrix()
     k_sides, v_sides = [[], []], [[], []]
     for h in (0, 1):
-        grad = mixed_grad[:, columns[h]]
+        grad, delta = scaled(h, SIDE)
         query = q_two[:, columns[h]]
         products = jnp.concatenate(
             [dot_nt(grad[first], kv_near[0, second, columns[h]]), dot_nt(grad[second], kv_near[3, second, columns[h]])], axis=0
         )
-        slopes = slopes_of(h, SIDE, products)
+        slopes = slopes_of(h, SIDE, products, delta)
         query_grads[h] = query_grads[h] + jnp.concatenate(
             [dot(slopes[first], kv_near[0, first, columns[h]]), dot(slopes[second], kv_near[3, first, columns[h]])], axis=0
         )
@@ -633,7 +640,7 @@
             vmem((2, 768, 2 * ROWS), BF16),
             vmem((2 * ROWS, HALF), F32),
             vmem((8, 8, ROWS), F32),
-            vmem((2 * ROWS, HALF), BF16),
+            vmem((2 * ROWS, HALF), F32),
             vmem((2 * ROWS, HALF), BF16),
             vmem((2 * ROWS, HALF), BF16),
             vmem((2, 2 * ROWS, HALF), BF16),

time: 45.4 us -> 45.4 us (level)
  no operation moved by 1% of the time
where the time goes in v2:
time: 45.4 us; the launch traced here: 45.3 us
  Pallas kernels  44.6 us (98%)
  between operations  0.64 us (1%)
    pallas_call x1, Pallas kernels, body(): pl.pallas_call(kernel, out_shape=(out, out, out, out), in_specs=[pl.Block...  43.8 us

profile of v2, /device:TPU:6, one launch (start us, length us, event | category | flops | bytes accessed | tf_op | source)
XLA Modules:
  0.0 45.3 jit_solution(5395928690913938553)
XLA Ops:
  0.6 43.8 %shard_map.93 = (bf16[128,512]{1,0:T(8,128)(2,1)S(1)}, bf16[128,512]{1,0:T(8,128)(2,1)S(1)}, bf16[128,512]{1,0:T(8,128)(2,1)S(1)}, bf16[128,512]{1,0:T(8,128)(2,1)S(1)}) custom-call(bf16[128,512]{1,0:T(8,128)(2,1)} %q_hbm.1, bf16[128,512]{1,0:T(8,128)(2,1)} %k_hbm.1, bf16[128,512]{1,0:T(8,128)(2,1)} %v_hbm.1, bf16[128,512]{1,0:T(8,128)(2,1)} %g_hbm.1, ...), custom_call_target="tpu_custom_call" | custom-call | flops 700000000 | bytes 1100000 | tf_op jit(solution)/shard_map/pallas_call | solution.py:618
  44.5 0.8 %shard_map.94 = (bf16[128,512]{1,0:T(8,128)(2,1)}, bf16[128,512]{1,0:T(8,128)(2,1)}, bf16[128,512]{1,0:T(8,128)(2,1)}, bf16[128,512]{1,0:T(8,128)(2,1)}) custom-call(bf16[128,512]{1,0:T(8,128)(2,1)S(1)} %get-tuple-element.8.refs_0_, bf16[128,512]{1,0:T(8,128)(2,1)S(1)} %get-tuple-element.9.refs_1_, bf16[128,512]{1,0:T(8,128)(2,1)S(1)} %get-tuple-element.10.refs_2_, ...), custom_call_target="tpu_custom_call" | custom-call | bytes 1100000 | tf_op jit(solution)/shard_map/pallas_call | solution.py:677

commit v3 on v2

--- a/solution.py
+++ b/solution.py
@@ -198,7 +198,7 @@
         for device in devices:
             pl.semaphore_signal(barrier, inc=1, device_id=device, device_id_type=MESH)
 
-    for steps in (2, -2, 1, -1):
+    for steps in (4, -4, 2, -2, 1, -1):
         when = inside(steps)
         only(when, lambda: greet([at(steps, 0), at(steps, 1)]))
         expected = expected + jnp.where(when[1], 2, 0)
@@ -223,6 +223,8 @@
                 two_recv.at[side, spot], at(steps * d, h), inside(sided=(steps,)),
             )
 
+    send_two(4, core, 5)
+    send_two(-4, other, 4)
     send_two(2, core, 1)
     send_two(-2, other, 0)
     for h in (0, 1):
@@ -319,15 +321,18 @@
 
     for side in (0, 1):
         sigma = direction(side)
-        pair, two = pl.ds(0, 2), -2 * sigma
+        four, two = -4 * sigma, -2 * sigma
+        for s in (4, 5):
+            arrived(two_in.at[side, s], two_recv.at[side, s], inside(four))
+        send(two_in.at[side, 5], two_in.at[side, 8], two_recv.at[side, 8], at(2 * sigma, core), inside(four, 2 * sigma))
+        send(
+            two_in.at[side, pl.ds(4, 2)], two_in.at[side, pl.ds(6, 2)],
+            two_recv.at[side, 6], at(sigma, core), inside(four, sigma),
+        )
         for s in (0, 1):
             arrived(two_in.at[side, s], two_recv.at[side, s], inside(two))
         send(
-            two_in.at[side, pair], two_in.at[side, pl.ds(4, 2)],
-            two_recv.at[side, 4], at(2 * sigma, core), inside(two, 2 * sigma),
-        )
-        send(
-            two_in.at[side, pair], two_in.at[side, pl.ds(2, 2)],
+            two_in.at[side, pl.ds(0, 2)], two_in.at[side, pl.ds(2, 2)],
             two_recv.at[side, 2], at(sigma, core), inside(two, sigma),
         )
 
@@ -339,16 +344,6 @@
     for h in (0, 1):
         scores = dot_nt(q_two[:, columns[h]], own_of(0, h)) * scale + near_bias[:, OWN]
         attend(h, OWN, scores, lambda e: dot(e, own_of(1, h)))
-
-    for side in (0, 1):
-        sigma = direction(side)
-        pair, four = pl.ds(4, 2), -4 * sigma
-        arrived(two_in.at[side, pair], two_recv.at[side, 4], inside(four))
-        send(
-            two_in.at[side, pair], two_in.at[side, pl.ds(6, 2)],
-            two_recv.at[side, 6], at(sigma, core), inside(four, sigma),
-        )
-        send(two_in.at[side, 5], two_in.at[side, 8], two_recv.at[side, 8], at(2 * sigma, core), inside(four, 2 * sigma))
 
     arrived(kv_near.at[3], near_recv.at[0], inside(1))
     arrived(kv_near.at[0], near_recv.at[1], inside(-1))

time: 45.4 us -> 45.1 us (level)
  Pallas kernels: 44.6 us -> 44 us
    pallas_call x1, Pallas kernels: 43.8 us -> 43.2 us  [body(): pl.pallas_call(kernel, out_shape=(out, out, out, out), in_specs=[pl.Block...]
where the time goes in v3:
time: 45.1 us; the launch traced here: 44.7 us
  Pallas kernels  44 us (98%)
  between operations  0.64 us (1%)
    pallas_call x1, Pallas kernels, body(): pl.pallas_call(kernel, out_shape=(out, out, out, out), in_specs=[pl.Block...  43.2 us

profile of v3, /device:TPU:6, one launch (start us, length us, event | category | flops | bytes accessed | tf_op | source)
XLA Modules:
  0.0 44.7 jit_solution(11765913194540947159)
XLA Ops:
  0.6 43.2 %shard_map.93 = (bf16[128,512]{1,0:T(8,128)(2,1)S(1)}, bf16[128,512]{1,0:T(8,128)(2,1)S(1)}, bf16[128,512]{1,0:T(8,128)(2,1)S(1)}, bf16[128,512]{1,0:T(8,128)(2,1)S(1)}) custom-call(bf16[128,512]{1,0:T(8,128)(2,1)} %q_hbm.1, bf16[128,512]{1,0:T(8,128)(2,1)} %k_hbm.1, bf16[128,512]{1,0:T(8,128)(2,1)} %v_hbm.1, bf16[128,512]{1,0:T(8,128)(2,1)} %g_hbm.1, ...), custom_call_target="tpu_custom_call" | custom-call | flops 700000000 | bytes 1100000 | tf_op jit(solution)/shard_map/pallas_call | solution.py:613
  43.8 0.8 %shard_map.94 = (bf16[128,512]{1,0:T(8,128)(2,1)}, bf16[128,512]{1,0:T(8,128)(2,1)}, bf16[128,512]{1,0:T(8,128)(2,1)}, bf16[128,512]{1,0:T(8,128)(2,1)}) custom-call(bf16[128,512]{1,0:T(8,128)(2,1)S(1)} %get-tuple-element.8.refs_0_, bf16[128,512]{1,0:T(8,128)(2,1)S(1)} %get-tuple-element.9.refs_1_, bf16[128,512]{1,0:T(8,128)(2,1)S(1)} %get-tuple-element.10.refs_2_, ...), custom_call_target="tpu_custom_call" | custom-call | bytes 1100000 | tf_op jit(solution)/shard_map/pallas_call | solution.py:672

commit v4 on v3

--- a/solution.py
+++ b/solution.py
@@ -97,9 +97,9 @@
     att_hbm, dq_hbm, dk_hbm, dv_hbm,
     kv_own, q_two, g_two, kv_near, pooled, one_in, two_in, k_middle, v_middle, k_last, v_last,
     level_s, frame_v, near_bias, far_bias, weight, turned, mixed, stats,
-    mixed_grad, att, dq, near_out, pool_out, two_out, sib_out, fold_out,
-    pass_in, four_in, fold_in, near_back, one_back, two_back, sib_back, dk, dv,
-    local_sem, send_sem, sib_recv, near_recv, one_recv, two_recv, stat_recv, pass_recv, fold_recv,
+    mixed_grad, att, dq, near_out, pool_out, two_out, sib_out,
+    pass_in, four_in, near_back, one_back, two_back, sib_back, dk, dv,
+    local_sem, send_sem, sib_recv, near_recv, one_recv, two_recv, stat_recv, pass_recv,
     back_near_recv, back_one_recv, back_two_recv, out_recv,
 ):
     blocks = lax.axis_size("seq")
@@ -166,7 +166,7 @@
 
     @pl.when((chip < 6) | (chip >= chips - 6))
     def _():
-        for ref in (one_in, two_in, pass_in, four_in, fold_in, near_back, one_back, two_back):
+        for ref in (one_in, two_in, pass_in, four_in, near_back, one_back, two_back):
             ref[...] = jnp.zeros(ref.shape, ref.dtype)
         for s in (0, 3):
             kv_near[s] = jnp.zeros(kv_near.shape[1:], BF16)
@@ -227,16 +227,21 @@
     send_two(-4, other, 4)
     send_two(2, core, 1)
     send_two(-2, other, 0)
+    send(kv_own.at[:, half(other)], kv_near.at[1 + core], sib_recv.at[0], sibling)
+    send(q_hbm.at[:, half(other)], q_two.at[mine], sib_recv.at[2], sibling)
+    for h in (0, 1):
+        send(kv_own.at[:, half(h)], kv_near.at[3 - 3 * core], near_recv.at[core], at(d, h), inside(sided=(1,)))
     for h in (0, 1):
         send(
             pooled.at[:, half(h)], one_in.at[core * 2 + 1],
             one_recv.at[core * 2 + 1], at(-d, h), inside(sided=(-1,)),
         )
-    send(kv_own.at[:, half(other)], kv_near.at[1 + core], sib_recv.at[0], sibling)
-    send(q_hbm.at[:, half(other)], q_two.at[mine], sib_recv.at[2], sibling)
-    for h in (0, 1):
-        send(kv_own.at[:, half(h)], kv_near.at[3 - 3 * core], near_recv.at[core], at(d, h), inside(sided=(1,)))
-    send(g_hbm.at[:, half(other)], g_two.at[mine], sib_recv.at[3], sibling)
+    ones_only = pl.ds(0, 2 * ONE)
+    for h in (0, 1):
+        send(
+            pooled.at[ones_only, half(h)], one_in.at[core * 2, ones_only],
+            one_recv.at[core * 2], at(2 * d, h), inside(sided=(2,)),
+        )
 
     locals_in[2].wait()
     locals_in[3].wait()
@@ -336,6 +341,8 @@
             two_recv.at[side, 2], at(sigma, core), inside(two, sigma),
         )
 
+    send(g_hbm.at[:, half(other)], g_two.at[mine], sib_recv.at[3], sibling)
+
     locals_in[4].wait()
     locals_in[6].wait()
     locals_in[5].wait()
@@ -347,15 +354,6 @@
 
     arrived(kv_near.at[3], near_recv.at[0], inside(1))
     arrived(kv_near.at[0], near_recv.at[1], inside(-1))
-    near_pools = [(dot(pool, kv_near[s, first]), dot(pool, kv_near[s, second])) for s in (0, 3)]
-    ones_only = pl.ds(0, 2 * ONE)
-    for i, side in ((0, 1), (1, 0)):
-        sigma = direction(side)
-        fold_out[i] = jnp.concatenate([p[:ONE] for p in near_pools[i]], axis=0).astype(BF16)
-        send(
-            fold_out.at[i], one_in.at[side * 2, ones_only],
-            one_recv.at[side * 2], at(sigma, core), inside(-sigma, sigma),
-        )
     for h in (0, 1):
         query = q_two[:, columns[h]]
         scores = jnp.concatenate(
@@ -368,6 +366,7 @@
             ),
         )
 
+    near_pools = [(dot(pool, kv_near[s, first]), dot(pool, kv_near[s, second])) for s in (0, 3)]
     for side in (0, 1):
         sigma = direction(side)
         arrived(one_in.at[side * 2, ones_only], one_recv.at[side * 2], inside(-2 * sigma))
@@ -380,8 +379,7 @@
         rows = slice(kind * TWO, (kind + 1) * TWO)
         for s in range(4):
             middle[s * ONE : (s + 1) * ONE] = one_in[s, ones]
-        for i in (0, 1):
-            middle[(4 + i) * ONE : (5 + i) * ONE] = fold_out[i, ones]
+        middle[4 * ONE : 6 * ONE] = jnp.concatenate([p[kind][:ONE] for p in near_pools], axis=0).astype(BF16)
         parts = [x[rows] for x in nearest] + [p[kind][ONE:] for p in near_pools]
         parts += [two_in[side, 0].astype(F32)[rows] for side in (0, 1)]
         middle[6 * ONE :] = jnp.concatenate(parts, axis=0).astype(BF16)
@@ -446,6 +444,10 @@
             deltas[h].append(jnp.sum(both[:, columns[h]], axis=1, keepdims=True))
     deltas = [jnp.concatenate(deltas[h], axis=0) for h in (0, 1)]
 
+    out_att = pltpu.make_async_copy(att.at[mine], att_hbm.at[:, half(core)], local_sem.at[8])
+    out_att.start()
+    send(att.at[theirs], att_hbm.at[:, half(core)], out_recv.at[0], sibling)
+
     unscale = 1.0 / math.sqrt(HEAD_DIM)
     query_grads = [None, None]
 
@@ -484,9 +486,6 @@
             two_out.at[side, pl.ds(1, 2)], pass_in.at[side, pl.ds(2, 2)],
             pass_recv.at[side, 1], at(-sigma, core), inside(-3 * sigma),
         )
-    out_att = pltpu.make_async_copy(att.at[mine], att_hbm.at[:, half(core)], local_sem.at[8])
-    out_att.start()
-    send(att.at[theirs], att_hbm.at[:, half(core)], out_recv.at[0], sibling)
 
     middle = plain_backward(MIDDLE, lambda h: k_middle[:, columns[h]], lambda h: v_middle[:, columns[h]])
     for s in range(4):
@@ -495,12 +494,12 @@
     for b in (0, 1):
         s = 2 * b + 1
         pool_out[s, 2 * ONE :] = two_rows(middle, 6 * ONE + s * TWO).astype(BF16)
-        send(pool_out.at[s], one_back.at[core], back_one_recv.at[core], at(direction(b), b), inside(direction(b)))
+        send(pool_out.at[s], one_back.at[core, 1], back_one_recv.at[core, 1], at(direction(b), b), inside(direction(b)))
     for side in (0, 1):
         sigma = direction(side)
         send(
-            pool_out.at[2 * side, ones_only], fold_in.at[side],
-            fold_recv.at[side], at(-sigma, core), inside(-2 * sigma),
+            pool_out.at[2 * side, ones_only], one_back.at[core, 0, ones_only],
+            back_one_recv.at[core, 0], at(-2 * sigma, side), inside(-2 * sigma),
         )
 
     spread = spread_matrix()
@@ -530,13 +529,10 @@
 
     for b in (0, 1):
         p = 5 - b
-        sigma = direction(b)
-        arrived(fold_in.at[b], fold_recv.at[b], inside(sigma, -sigma))
-        folded = fold_in[b].astype(F32)
         for kind, sides in ((0, k_sides), (1, v_sides)):
             pools = middle[kind]
             small = jnp.concatenate(
-                [pools[p * ONE : (p + 1) * ONE] + folded[kind * ONE : (kind + 1) * ONE], pools[6 * ONE + p * TWO : 6 * ONE + (p + 1) * TWO]], axis=0
+                [pools[p * ONE : (p + 1) * ONE], pools[6 * ONE + p * TWO : 6 * ONE + (p + 1) * TWO]], axis=0
             )
             near_out[b, kind * ROWS : (kind + 1) * ROWS] = (
                 jnp.concatenate(sides[b], axis=1) + dot(spread, small.astype(BF16))
@@ -544,15 +540,6 @@
         send(near_out.at[b], near_back.at[core], back_near_recv.at[core], at(-direction(b), b), inside(-direction(b)))
 
     own = plain_backward(OWN, lambda h: own_of(0, h), lambda h: own_of(1, h))
-    for kind in (0, 1):
-        sib_out[kind * ROWS : (kind + 1) * ROWS] = jnp.where(core == 0, own[kind][second], own[kind][first]).astype(BF16)
-    send(sib_out, sib_back, out_recv.at[1], sibling)
-    for h in (0, 1):
-        dq[:, columns[h]] = (query_grads[h] * unscale).astype(BF16)
-    out_dq = pltpu.make_async_copy(dq.at[mine], dq_hbm.at[:, half(core)], local_sem.at[9])
-    out_dq.start()
-    send(dq.at[theirs], dq_hbm.at[:, half(core)], out_recv.at[2], sibling)
-
     for side in (0, 1):
         sigma = direction(side)
         two = -2 * sigma
@@ -564,15 +551,26 @@
         send(two_out.at[side, 0], two_back.at[core, 0], back_two_recv.at[core, 0], at(two, 1 - side), inside(two))
         send(two_out.at[side, 8], two_back.at[core, 1], back_two_recv.at[core, 1], at(two, side), inside(two))
 
+    for kind in (0, 1):
+        sib_out[kind * ROWS : (kind + 1) * ROWS] = jnp.where(core == 0, own[kind][second], own[kind][first]).astype(BF16)
+    send(sib_out, sib_back, out_recv.at[1], sibling)
+    for h in (0, 1):
+        dq[:, columns[h]] = (query_grads[h] * unscale).astype(BF16)
+    out_dq = pltpu.make_async_copy(dq.at[mine], dq_hbm.at[:, half(core)], local_sem.at[9])
+    out_dq.start()
+    send(dq.at[theirs], dq_hbm.at[:, half(core)], out_recv.at[2], sibling)
+
     arrived(sib_back, out_recv.at[1])
     mine_grads = [jnp.where(core == 0, own[kind][first], own[kind][second]) for kind in (0, 1)]
     bases = {}
     for h in (0, 1):
-        arrived(one_back.at[h], back_one_recv.at[h], inside(sided=(-1,)))
+        arrived(one_back.at[h, 0, ones_only], back_one_recv.at[h, 0], inside(sided=(2,)))
+        arrived(one_back.at[h, 1], back_one_recv.at[h, 1], inside(sided=(-1,)))
         for j, steps in enumerate((-2, 2)):
             arrived(two_back.at[h, j], back_two_recv.at[h, j], inside(sided=(steps,)))
-        ones = one_back[h].astype(F32)
+        ones = one_back[h, 1].astype(F32)
         twos = ones[2 * ONE :] + two_back[h, 0].astype(F32) + two_back[h, 1].astype(F32)
+        ones = ones[: 2 * ONE] + one_back[h, 0, : 2 * ONE].astype(F32)
         for kind in (0, 1):
             rows = slice(kind * ROWS, (kind + 1) * ROWS)
             small = jnp.concatenate([ones[kind * ONE : (kind + 1) * ONE], twos[kind * TWO : (kind + 1) * TWO]], axis=0)
@@ -642,12 +640,10 @@
             vmem((4, POOLED, HALF), BF16),
             vmem((2, 9, 2 * TWO, HALF), BF16),
             vmem((2 * ROWS, HALF), BF16),
-            vmem((2, 2 * ONE, HALF), BF16),
             vmem((2, 5, 2 * TWO, HALF), BF16),
             vmem((2, 2, 2 * TWO, HALF), BF16),
-            vmem((2, 2 * ONE, HALF), BF16),
             vmem((2, 2 * ROWS, HALF), BF16),
-            vmem((2, POOLED, HALF), BF16),
+            vmem((2, 2, POOLED, HALF), BF16),
             vmem((2, 2, 2 * TWO, HALF), BF16),
             vmem((2 * ROWS, HALF), BF16),
             vmem((ROWS, width), BF16),
@@ -661,8 +657,7 @@
             dma((8,)),
             dma((2, 4)),
             dma((2,)),
-            dma((2,)),
-            dma((2,)),
+            dma((2, 2)),
             dma((2, 2)),
             dma((3,)),
         ],

time: 45.1 us -> 45.2 us (level)
  no operation moved by 1% of the time
where the time goes in v4:
time: 45.2 us; the launch traced here: 44.4 us
  Pallas kernels  43.7 us (97%)
  between operations  0.64 us (1%)
    pallas_call x1, Pallas kernels, body(): pl.pallas_call(kernel, out_shape=(out, out, out, out), in_specs=[pl.Block...  42.9 us

profile of v4, /device:TPU:6, one launch (start us, length us, event | category | flops | bytes accessed | tf_op | source)
XLA Modules:
  0.0 44.4 jit_solution(6658326430097959938)
XLA Ops:
  0.6 42.9 %shard_map.93 = (bf16[128,512]{1,0:T(8,128)(2,1)S(1)}, bf16[128,512]{1,0:T(8,128)(2,1)S(1)}, bf16[128,512]{1,0:T(8,128)(2,1)S(1)}, bf16[128,512]{1,0:T(8,128)(2,1)S(1)}) custom-call(bf16[128,512]{1,0:T(8,128)(2,1)} %q_hbm.1, bf16[128,512]{1,0:T(8,128)(2,1)} %k_hbm.1, bf16[128,512]{1,0:T(8,128)(2,1)} %v_hbm.1, bf16[128,512]{1,0:T(8,128)(2,1)} %g_hbm.1, ...), custom_call_target="tpu_custom_call" | custom-call | flops 700000000 | bytes 1100000 | tf_op jit(solution)/shard_map/pallas_call | solution.py:611
  43.6 0.8 %shard_map.94 = (bf16[128,512]{1,0:T(8,128)(2,1)}, bf16[128,512]{1,0:T(8,128)(2,1)}, bf16[128,512]{1,0:T(8,128)(2,1)}, bf16[128,512]{1,0:T(8,128)(2,1)}) custom-call(bf16[128,512]{1,0:T(8,128)(2,1)S(1)} %get-tuple-element.8.refs_0_, bf16[128,512]{1,0:T(8,128)(2,1)S(1)} %get-tuple-element.9.refs_1_, bf16[128,512]{1,0:T(8,128)(2,1)S(1)} %get-tuple-element.10.refs_2_, ...), custom_call_target="tpu_custom_call" | custom-call | bytes 1100000 | tf_op jit(solution)/shard_map/pallas_call | solution.py:667

commit v5 on v4

--- a/solution.py
+++ b/solution.py
@@ -148,11 +148,12 @@
         only(when, copy.start)
         started.append((copy, when))
 
-    def flush():
+    def flush(keep=0):
         groups = {}
-        for copy, when in started:
+        done = len(started) - keep
+        for copy, when in started[:done]:
             groups.setdefault(when and when[0], (when, []))[1].append(copy)
-        started.clear()
+        del started[:done]
         for when, copies in groups.values():
 
             def wait_all(copies=copies):
@@ -424,6 +425,7 @@
             factors[h].append(jnp.exp2(highs[h][index] - highs[h][-1]) * inverse_totals[h])
             if part in (MIDDLE, LAST):
                 turned[h, part, :] = weight[h, :, part].astype(BF16).T
+    flush(keep=mates - 1)
     for k in range(1, mates):
         source = (place + k) % mates
         arrived(stats.at[source], stat_recv.at[source])
@@ -540,6 +542,7 @@
         send(near_out.at[b], near_back.at[core], back_near_recv.at[core], at(-direction(b), b), inside(-direction(b)))
 
     own = plain_backward(OWN, lambda h: own_of(0, h), lambda h: own_of(1, h))
+    flush(keep=2)
     for side in (0, 1):
         sigma = direction(side)
         two = -2 * sigma
@@ -560,34 +563,36 @@
     out_dq.start()
     send(dq.at[theirs], dq_hbm.at[:, half(core)], out_recv.at[2], sibling)
 
-    arrived(sib_back, out_recv.at[1])
-    mine_grads = [jnp.where(core == 0, own[kind][first], own[kind][second]) for kind in (0, 1)]
-    bases = {}
-    for h in (0, 1):
+    outs = [out_att, out_dq]
+
+    def finish(h, sem, rest):
         arrived(one_back.at[h, 0, ones_only], back_one_recv.at[h, 0], inside(sided=(2,)))
         arrived(one_back.at[h, 1], back_one_recv.at[h, 1], inside(sided=(-1,)))
+        arrived(near_back.at[h], back_near_recv.at[h], inside(sided=(1,)))
         for j, steps in enumerate((-2, 2)):
             arrived(two_back.at[h, j], back_two_recv.at[h, j], inside(sided=(steps,)))
         ones = one_back[h, 1].astype(F32)
         twos = ones[2 * ONE :] + two_back[h, 0].astype(F32) + two_back[h, 1].astype(F32)
         ones = ones[: 2 * ONE] + one_back[h, 0, : 2 * ONE].astype(F32)
-        for kind in (0, 1):
-            rows = slice(kind * ROWS, (kind + 1) * ROWS)
+        sums = []
+        for kind, rows in ((0, first), (1, second)):
             small = jnp.concatenate([ones[kind * ONE : (kind + 1) * ONE], twos[kind * TWO : (kind + 1) * TWO]], axis=0)
-            grads = jnp.where(core == h, mine_grads[kind], sib_back[rows].astype(F32))
-            bases[h, kind] = grads + dot(spread, small.astype(BF16))
+            sums.append(near_back[h, rows].astype(F32) + dot(spread, small.astype(BF16)))
+        rest = rest()
+        for kind, out, out_hbm in ((0, dk, dk_hbm), (1, dv, dv_hbm)):
+            out[:, half(h)] = (sums[kind] + rest[kind]).astype(BF16)
+            outs.append(pltpu.make_async_copy(out.at[:, half(h)], out_hbm.at[:, half(h)], local_sem.at[sem + kind]))
+            outs[-1].start()
+
+    def from_sibling():
+        arrived(sib_back, out_recv.at[1])
+        return [sib_back[rows].astype(F32) for rows in (first, second)]
+
+    finish(core, 10, lambda: [jnp.where(core == 0, own[kind][first], own[kind][second]) for kind in (0, 1)])
+    finish(other, 12, from_sibling)
     arrived(att_hbm.at[:, half(other)], out_recv.at[0])
     arrived(dq_hbm.at[:, half(other)], out_recv.at[2])
     flush()
-    for h in (0, 1):
-        arrived(near_back.at[h], back_near_recv.at[h], inside(sided=(1,)))
-    outs = [out_att, out_dq]
-    for kind, out, out_hbm in ((0, dk, dk_hbm), (1, dv, dv_hbm)):
-        rows = slice(kind * ROWS, (kind + 1) * ROWS)
-        for h in (0, 1):
-            out[:, h * HALF : (h + 1) * HALF] = (bases[h, kind] + near_back[h, rows].astype(F32)).astype(BF16)
-        outs.append(pltpu.make_async_copy(out, out_hbm, local_sem.at[10 + kind]))
-        outs[-1].start()
     for copy in outs:
         copy.wait()
 
@@ -648,7 +653,7 @@
             vmem((2 * ROWS, HALF), BF16),
             vmem((ROWS, width), BF16),
             vmem((ROWS, width), BF16),
-            dma((12,)),
+            dma((14,)),
             dma((64,)),
             dma((5,)),
             dma((2,)),

time: 45.2 us -> 44.6 us (0.987)
  no operation moved by 1% of the time
where the time goes in v5:
time: 44.6 us; the launch traced here: 44 us
  Pallas kernels  43.3 us (97%)
  between operations  0.64 us (1%)
    pallas_call x1, Pallas kernels, body(): pl.pallas_call(kernel, out_shape=(out, out, out, out), in_specs=[pl.Block...  42.5 us

profile of v5, /device:TPU:6, one launch (start us, length us, event | category | flops | bytes accessed | tf_op | source)
XLA Modules:
  0.0 44.0 jit_solution(9861968976356954564)
XLA Ops:
  0.6 42.5 %shard_map.93 = (bf16[128,512]{1,0:T(8,128)(2,1)S(1)}, bf16[128,512]{1,0:T(8,128)(2,1)S(1)}, bf16[128,512]{1,0:T(8,128)(2,1)S(1)}, bf16[128,512]{1,0:T(8,128)(2,1)S(1)}) custom-call(bf16[128,512]{1,0:T(8,128)(2,1)} %q_hbm.1, bf16[128,512]{1,0:T(8,128)(2,1)} %k_hbm.1, bf16[128,512]{1,0:T(8,128)(2,1)} %v_hbm.1, bf16[128,512]{1,0:T(8,128)(2,1)} %g_hbm.1, ...), custom_call_target="tpu_custom_call" | custom-call | flops 700000000 | bytes 1100000 | tf_op jit(solution)/shard_map/pallas_call | solution.py:616
  43.1 0.8 %shard_map.94 = (bf16[128,512]{1,0:T(8,128)(2,1)}, bf16[128,512]{1,0:T(8,128)(2,1)}, bf16[128,512]{1,0:T(8,128)(2,1)}, bf16[128,512]{1,0:T(8,128)(2,1)}) custom-call(bf16[128,512]{1,0:T(8,128)(2,1)S(1)} %get-tuple-element.8.refs_0_, bf16[128,512]{1,0:T(8,128)(2,1)S(1)} %get-tuple-element.9.refs_1_, bf16[128,512]{1,0:T(8,128)(2,1)S(1)} %get-tuple-element.10.refs_2_, ...), custom_call_target="tpu_custom_call" | custom-call | bytes 1100000 | tf_op jit(solution)/shard_map/pallas_call | solution.py:672

commit v6 on v5

--- a/solution.py
+++ b/solution.py
@@ -148,6 +148,20 @@
         only(when, copy.start)
         started.append((copy, when))
 
+    def send_all(copies, when):
+        nonlocal sent
+        made = []
+        for src, dst, recv, device in copies:
+            made.append(remote(src, dst, send_sem.at[sent], recv, device))
+            sent += 1
+
+        def start_all():
+            for copy in made:
+                copy.start()
+
+        only(when, start_all)
+        started.extend((copy, when) for copy in made)
+
     def flush(keep=0):
         groups = {}
         done = len(started) - keep
@@ -164,6 +178,13 @@
 
     def arrived(ref, sem, when=None):
         only(when, remote(ref, ref, sem, sem, sibling).wait_recv)
+
+    def all_arrived(pairs, when):
+        def wait_all():
+            for ref, sem in pairs:
+                arrived(ref, sem)
+
+        only(when, wait_all)
 
     @pl.when((chip < 6) | (chip >= chips - 6))
     def _():
@@ -217,12 +238,16 @@
 
     pl.semaphore_wait(barrier, expected)
 
+    two_rows_out = pl.ds(2 * ONE, 2 * TWO)
+
     def send_two(steps, side, spot):
-        for h in (0, 1):
-            send(
-                pooled.at[pl.ds(2 * ONE, 2 * TWO), half(h)], two_in.at[side, spot],
-                two_recv.at[side, spot], at(steps * d, h), inside(sided=(steps,)),
-            )
+        send_all(
+            [
+                (pooled.at[two_rows_out, half(h)], two_in.at[side, spot], two_recv.at[side, spot], at(steps * d, h))
+                for h in (0, 1)
+            ],
+            inside(sided=(steps,)),
+        )
 
     send_two(4, core, 5)
     send_two(-4, other, 4)
@@ -230,19 +255,23 @@
     send_two(-2, other, 0)
     send(kv_own.at[:, half(other)], kv_near.at[1 + core], sib_recv.at[0], sibling)
     send(q_hbm.at[:, half(other)], q_two.at[mine], sib_recv.at[2], sibling)
-    for h in (0, 1):
-        send(kv_own.at[:, half(h)], kv_near.at[3 - 3 * core], near_recv.at[core], at(d, h), inside(sided=(1,)))
-    for h in (0, 1):
-        send(
-            pooled.at[:, half(h)], one_in.at[core * 2 + 1],
-            one_recv.at[core * 2 + 1], at(-d, h), inside(sided=(-1,)),
-        )
     ones_only = pl.ds(0, 2 * ONE)
-    for h in (0, 1):
-        send(
-            pooled.at[ones_only, half(h)], one_in.at[core * 2, ones_only],
-            one_recv.at[core * 2], at(2 * d, h), inside(sided=(2,)),
-        )
+    send_all(
+        [(kv_own.at[:, half(h)], kv_near.at[3 - 3 * core], near_recv.at[core], at(d, h)) for h in (0, 1)],
+        inside(sided=(1,)),
+    )
+    spot_one = core * 2
+    send_all(
+        [(pooled.at[:, half(h)], one_in.at[spot_one + 1], one_recv.at[spot_one + 1], at(-d, h)) for h in (0, 1)],
+        inside(sided=(-1,)),
+    )
+    send_all(
+        [
+            (pooled.at[ones_only, half(h)], one_in.at[spot_one, ones_only], one_recv.at[spot_one], at(2 * d, h))
+            for h in (0, 1)
+        ],
+        inside(sided=(2,)),
+    )
 
     locals_in[2].wait()
     locals_in[3].wait()
@@ -328,15 +357,13 @@
     for side in (0, 1):
         sigma = direction(side)
         four, two = -4 * sigma, -2 * sigma
-        for s in (4, 5):
-            arrived(two_in.at[side, s], two_recv.at[side, s], inside(four))
+        all_arrived([(two_in.at[side, s], two_recv.at[side, s]) for s in (4, 5)], inside(four))
         send(two_in.at[side, 5], two_in.at[side, 8], two_recv.at[side, 8], at(2 * sigma, core), inside(four, 2 * sigma))
         send(
             two_in.at[side, pl.ds(4, 2)], two_in.at[side, pl.ds(6, 2)],
             two_recv.at[side, 6], at(sigma, core), inside(four, sigma),
         )
-        for s in (0, 1):
-            arrived(two_in.at[side, s], two_recv.at[side, s], inside(two))
+        all_arrived([(two_in.at[side, s], two_recv.at[side, s]) for s in (0, 1)], inside(two))
         send(
             two_in.at[side, pl.ds(0, 2)], two_in.at[side, pl.ds(2, 2)],
             two_recv.at[side, 2], at(sigma, core), inside(two, sigma),
@@ -599,7 +626,12 @@
 
 def write_out(*refs):
     *arrays, sems = refs
-    copies = [pltpu.make_async_copy(arrays[i], arrays[4 + i], sems.at[i]) for i in range(4)]
+    rows = arrays[0].shape[0] // 2
+    copies = []
+    for i in range(4):
+        for j in (0, 1):
+            part = pl.ds(j * rows, rows)
+            copies.append(pltpu.make_async_copy(arrays[i].at[part], arrays[4 + i].at[part], sems.at[2 * i + j]))
     for copy in copies:
         copy.start()
     for copy in copies:
@@ -674,7 +706,7 @@
         out_shape=(out, out, out, out),
         in_specs=[pl.BlockSpec(memory_space=pl.ANY)] * 4,
         out_specs=(pl.BlockSpec(memory_space=pl.ANY),) * 4,
-        scratch_shapes=[dma((4,))],
+        scratch_shapes=[dma((8,))],
         compiler_params=pltpu.CompilerParams(vmem_limit_bytes=limit),
         cost_estimate=pl.CostEstimate(flops=0, bytes_accessed=1_100_000, transcendentals=0),
     )(*results)

time: 44.6 us -> 44.6 us (level)
  no operation moved by 1% of the time
where the time goes in v6:
time: 44.6 us; the launch traced here: 44 us
  Pallas kernels  43.3 us (97%)
  between operations  0.64 us (1%)
    pallas_call x1, Pallas kernels, body(): pl.pallas_call(kernel, out_shape=(out, out, out, out), in_specs=[pl.Block...  42.5 us

profile of v6, /device:TPU:6, one launch (start us, length us, event | category | flops | bytes accessed | tf_op | source)
XLA Modules:
  0.0 44.0 jit_solution(4739629796441489934)
XLA Ops:
  0.6 42.5 %shard_map.93 = (bf16[128,512]{1,0:T(8,128)(2,1)S(1)}, bf16[128,512]{1,0:T(8,128)(2,1)S(1)}, bf16[128,512]{1,0:T(8,128)(2,1)S(1)}, bf16[128,512]{1,0:T(8,128)(2,1)S(1)}) custom-call(bf16[128,512]{1,0:T(8,128)(2,1)} %q_hbm.1, bf16[128,512]{1,0:T(8,128)(2,1)} %k_hbm.1, bf16[128,512]{1,0:T(8,128)(2,1)} %v_hbm.1, bf16[128,512]{1,0:T(8,128)(2,1)} %g_hbm.1, ...), custom_call_target="tpu_custom_call" | custom-call | flops 700000000 | bytes 1100000 | tf_op jit(solution)/shard_map/pallas_call | solution.py:648
  43.1 0.9 %shard_map.94 = (bf16[128,512]{1,0:T(8,128)(2,1)}, bf16[128,512]{1,0:T(8,128)(2,1)}, bf16[128,512]{1,0:T(8,128)(2,1)}, bf16[128,512]{1,0:T(8,128)(2,1)}) custom-call(bf16[128,512]{1,0:T(8,128)(2,1)S(1)} %get-tuple-element.8.refs_0_, bf16[128,512]{1,0:T(8,128)(2,1)S(1)} %get-tuple-element.9.refs_1_, bf16[128,512]{1,0:T(8,128)(2,1)S(1)} %get-tuple-element.10.refs_2_, ...), custom_call_target="tpu_custom_call" | custom-call | bytes 1100000 | tf_op jit(solution)/shard_map/pallas_call | solution.py:704

commit v7 on v5

--- a/solution.py
+++ b/solution.py
@@ -98,7 +98,7 @@
     kv_own, q_two, g_two, kv_near, pooled, one_in, two_in, k_middle, v_middle, k_last, v_last,
     level_s, frame_v, near_bias, far_bias, weight, turned, mixed, stats,
     mixed_grad, att, dq, near_out, pool_out, two_out, sib_out,
-    pass_in, four_in, near_back, one_back, two_back, sib_back, dk, dv,
+    pass_in, near_back, one_back, two_back, sib_back, dk, dv,
     local_sem, send_sem, sib_recv, near_recv, one_recv, two_recv, stat_recv, pass_recv,
     back_near_recv, back_one_recv, back_two_recv, out_recv,
 ):
@@ -167,7 +167,7 @@
 
     @pl.when((chip < 6) | (chip >= chips - 6))
     def _():
-        for ref in (one_in, two_in, pass_in, four_in, near_back, one_back, two_back):
+        for ref in (one_in, two_in, pass_in, near_back, one_back, two_back):
             ref[...] = jnp.zeros(ref.shape, ref.dtype)
         for s in (0, 3):
             kv_near[s] = jnp.zeros(kv_near.shape[1:], BF16)
@@ -521,13 +521,20 @@
             v_sides[b].append(dot(turned[h, SIDE, rows], grad[rows]))
     for side in (0, 1):
         sigma = direction(side)
-        four = -4 * sigma
+        four, two = -4 * sigma, -2 * sigma
         arrived(pass_in.at[side, pl.ds(0, 2)], pass_recv.at[side, 0], inside(sigma, four))
         arrived(pass_in.at[side, 4], pass_recv.at[side, 2], inside(2 * sigma, four))
-        passed = [pass_in[side, s].astype(F32) for s in (0, 1, 4)]
+        arrived(pass_in.at[side, pl.ds(2, 2)], pass_recv.at[side, 1], inside(sigma, two))
+        passed = pass_in[side].astype(F32)
         two_out[side, 3] = (two_rows(last, (side * 7 + 2) * TWO) + passed[0]).astype(BF16)
-        two_out[side, 4] = (two_rows(last, (side * 7 + 3) * TWO) + passed[1] + passed[2]).astype(BF16)
-        send(two_out.at[side, pl.ds(3, 2)], four_in.at[side], pass_recv.at[side, 3], at(-2 * sigma, core), inside(four))
+        two_out[side, 4] = (two_rows(last, (side * 7 + 3) * TWO) + passed[1] + passed[4]).astype(BF16)
+        two_out[side, 0] = (two_rows(middle, 6 * ONE + (6 + side) * TWO) + passed[2]).astype(BF16)
+        two_out[side, 8] = (two_rows(middle, 6 * ONE + 2 * side * TWO) + passed[3]).astype(BF16)
+        for s, spot, owner, steps in ((3, 2, 1 - side, four), (4, 3, side, four), (0, 0, 1 - side, two), (8, 1, side, two)):
+            send(
+                two_out.at[side, s], two_back.at[core, spot],
+                back_two_recv.at[core, spot], at(steps, owner), inside(steps),
+            )
 
     for b in (0, 1):
         p = 5 - b
@@ -542,18 +549,6 @@
         send(near_out.at[b], near_back.at[core], back_near_recv.at[core], at(-direction(b), b), inside(-direction(b)))
 
     own = plain_backward(OWN, lambda h: own_of(0, h), lambda h: own_of(1, h))
-    flush(keep=2)
-    for side in (0, 1):
-        sigma = direction(side)
-        two = -2 * sigma
-        arrived(pass_in.at[side, pl.ds(2, 2)], pass_recv.at[side, 1], inside(sigma, two))
-        arrived(four_in.at[side], pass_recv.at[side, 3], inside(2 * sigma, two))
-        passed = pass_in[side, 2:4].astype(F32) + four_in[side].astype(F32)
-        two_out[side, 0] = (two_rows(middle, 6 * ONE + (6 + side) * TWO) + passed[0]).astype(BF16)
-        two_out[side, 8] = (two_rows(middle, 6 * ONE + 2 * side * TWO) + passed[1]).astype(BF16)
-        send(two_out.at[side, 0], two_back.at[core, 0], back_two_recv.at[core, 0], at(two, 1 - side), inside(two))
-        send(two_out.at[side, 8], two_back.at[core, 1], back_two_recv.at[core, 1], at(two, side), inside(two))
-
     for kind in (0, 1):
         sib_out[kind * ROWS : (kind + 1) * ROWS] = jnp.where(core == 0, own[kind][second], own[kind][first]).astype(BF16)
     send(sib_out, sib_back, out_recv.at[1], sibling)
@@ -563,16 +558,19 @@
     out_dq.start()
     send(dq.at[theirs], dq_hbm.at[:, half(core)], out_recv.at[2], sibling)
 
+    flush(keep=4)
     outs = [out_att, out_dq]
 
     def finish(h, sem, rest):
         arrived(one_back.at[h, 0, ones_only], back_one_recv.at[h, 0], inside(sided=(2,)))
         arrived(one_back.at[h, 1], back_one_recv.at[h, 1], inside(sided=(-1,)))
         arrived(near_back.at[h], back_near_recv.at[h], inside(sided=(1,)))
-        for j, steps in enumerate((-2, 2)):
+        for j, steps in enumerate((-2, 2, -4, 4)):
             arrived(two_back.at[h, j], back_two_recv.at[h, j], inside(sided=(steps,)))
         ones = one_back[h, 1].astype(F32)
-        twos = ones[2 * ONE :] + two_back[h, 0].astype(F32) + two_back[h, 1].astype(F32)
+        twos = ones[2 * ONE :]
+        for j in range(4):
+            twos = twos + two_back[h, j].astype(F32)
         ones = ones[: 2 * ONE] + one_back[h, 0, : 2 * ONE].astype(F32)
         sums = []
         for kind, rows in ((0, first), (1, second)):
@@ -646,10 +644,9 @@
             vmem((2, 9, 2 * TWO, HALF), BF16),
             vmem((2 * ROWS, HALF), BF16),
             vmem((2, 5, 2 * TWO, HALF), BF16),
-            vmem((2, 2, 2 * TWO, HALF), BF16),
             vmem((2, 2 * ROWS, HALF), BF16),
             vmem((2, 2, POOLED, HALF), BF16),
-            vmem((2, 2, 2 * TWO, HALF), BF16),
+            vmem((2, 4, 2 * TWO, HALF), BF16),
             vmem((2 * ROWS, HALF), BF16),
             vmem((ROWS, width), BF16),
             vmem((ROWS, width), BF16),
@@ -660,10 +657,10 @@
             dma((4,)),
             dma((2, 9)),
             dma((8,)),
-            dma((2, 4)),
+            dma((2, 3)),
             dma((2,)),
             dma((2, 2)),
-            dma((2, 2)),
+            dma((2, 4)),
             dma((3,)),
         ],
         compiler_params=pltpu.CompilerParams(collective_id=0, has_side_effects=True, vmem_limit_bytes=limit),

time: 44.6 us -> 44.1 us (0.989); the launches traced: 44 us -> 44 us
  no operation moved by 1% of the time
where the time goes in v7:
time: 44.1 us; the launch traced here: 44 us
  Pallas kernels  43.4 us (98%)
  between operations  0.64 us (1%)
    pallas_call x1, Pallas kernels, body(): pl.pallas_call(kernel, out_shape=(out, out, out, out), in_specs=[pl.Block...  42.5 us

profile of v7, /device:TPU:6, one launch (start us, length us, event | category | flops | bytes accessed | tf_op | source)
XLA Modules:
  0.0 44.0 jit_solution(1544734200353034563)
XLA Ops:
  0.6 42.5 %shard_map.93 = (bf16[128,512]{1,0:T(8,128)(2,1)S(1)}, bf16[128,512]{1,0:T(8,128)(2,1)S(1)}, bf16[128,512]{1,0:T(8,128)(2,1)S(1)}, bf16[128,512]{1,0:T(8,128)(2,1)S(1)}) custom-call(bf16[128,512]{1,0:T(8,128)(2,1)} %q_hbm.1, bf16[128,512]{1,0:T(8,128)(2,1)} %k_hbm.1, bf16[128,512]{1,0:T(8,128)(2,1)} %v_hbm.1, bf16[128,512]{1,0:T(8,128)(2,1)} %g_hbm.1, ...), custom_call_target="tpu_custom_call" | custom-call | flops 700000000 | bytes 1100000 | tf_op jit(solution)/shard_map/pallas_call | solution.py:614
  43.2 0.8 %shard_map.94 = (bf16[128,512]{1,0:T(8,128)(2,1)}, bf16[128,512]{1,0:T(8,128)(2,1)}, bf16[128,512]{1,0:T(8,128)(2,1)}, bf16[128,512]{1,0:T(8,128)(2,1)}) custom-call(bf16[128,512]{1,0:T(8,128)(2,1)S(1)} %get-tuple-element.8.refs_0_, bf16[128,512]{1,0:T(8,128)(2,1)S(1)} %get-tuple-element.9.refs_1_, bf16[128,512]{1,0:T(8,128)(2,1)S(1)} %get-tuple-element.10.refs_2_, ...), custom_call_target="tpu_custom_call" | custom-call | bytes 1100000 | tf_op jit(solution)/shard_map/pallas_call | solution.py:669

commit v8 on v7

--- a/solution.py
+++ b/solution.py
@@ -519,6 +519,18 @@
         for b, rows in ((0, second), (1, first)):
             k_sides[b].append(dot_tn(slopes[rows], query[rows]) * unscale)
             v_sides[b].append(dot(turned[h, SIDE, rows], grad[rows]))
+    for b in (0, 1):
+        p = 5 - b
+        for kind, sides in ((0, k_sides), (1, v_sides)):
+            pools = middle[kind]
+            small = jnp.concatenate(
+                [pools[p * ONE : (p + 1) * ONE], pools[6 * ONE + p * TWO : 6 * ONE + (p + 1) * TWO]], axis=0
+            )
+            near_out[b, kind * ROWS : (kind + 1) * ROWS] = (
+                jnp.concatenate(sides[b], axis=1) + dot(spread, small.astype(BF16))
+            ).astype(BF16)
+        send(near_out.at[b], near_back.at[core], back_near_recv.at[core], at(-direction(b), b), inside(-direction(b)))
+
     for side in (0, 1):
         sigma = direction(side)
         four, two = -4 * sigma, -2 * sigma
@@ -535,18 +547,6 @@
                 two_out.at[side, s], two_back.at[core, spot],
                 back_two_recv.at[core, spot], at(steps, owner), inside(steps),
             )
-
-    for b in (0, 1):
-        p = 5 - b
-        for kind, sides in ((0, k_sides), (1, v_sides)):
-            pools = middle[kind]
-            small = jnp.concatenate(
-                [pools[p * ONE : (p + 1) * ONE], pools[6 * ONE + p * TWO : 6 * ONE + (p + 1) * TWO]], axis=0
-            )
-            near_out[b, kind * ROWS : (kind + 1) * ROWS] = (
-                jnp.concatenate(sides[b], axis=1) + dot(spread, small.astype(BF16))
-            ).astype(BF16)
-        send(near_out.at[b], near_back.at[core], back_near_recv.at[core], at(-direction(b), b), inside(-direction(b)))
 
     own = plain_backward(OWN, lambda h: own_of(0, h), lambda h: own_of(1, h))
     for kind in (0, 1):

time: 44.1 us -> 44.2 us (level)
  no operation moved by 1% of the time
where the time goes in v8:
time: 44.2 us; the launch traced here: 44 us
  Pallas kernels  43.4 us (98%)
  between operations  0.64 us (1%)
    pallas_call x1, Pallas kernels, body(): pl.pallas_call(kernel, out_shape=(out, out, out, out), in_specs=[pl.Block...  42.6 us

profile of v8, /device:TPU:6, one launch (start us, length us, event | category | flops | bytes accessed | tf_op | source)
XLA Modules:
  0.0 44.0 jit_solution(10928997392751723221)
XLA Ops:
  0.6 42.6 %shard_map.93 = (bf16[128,512]{1,0:T(8,128)(2,1)S(1)}, bf16[128,512]{1,0:T(8,128)(2,1)S(1)}, bf16[128,512]{1,0:T(8,128)(2,1)S(1)}, bf16[128,512]{1,0:T(8,128)(2,1)S(1)}) custom-call(bf16[128,512]{1,0:T(8,128)(2,1)} %q_hbm.1, bf16[128,512]{1,0:T(8,128)(2,1)} %k_hbm.1, bf16[128,512]{1,0:T(8,128)(2,1)} %v_hbm.1, bf16[128,512]{1,0:T(8,128)(2,1)} %g_hbm.1, ...), custom_call_target="tpu_custom_call" | custom-call | flops 700000000 | bytes 1100000 | tf_op jit(solution)/shard_map/pallas_call | solution.py:614
  43.2 0.8 %shard_map.94 = (bf16[128,512]{1,0:T(8,128)(2,1)}, bf16[128,512]{1,0:T(8,128)(2,1)}, bf16[128,512]{1,0:T(8,128)(2,1)}, bf16[128,512]{1,0:T(8,128)(2,1)}) custom-call(bf16[128,512]{1,0:T(8,128)(2,1)S(1)} %get-tuple-element.8.refs_0_, bf16[128,512]{1,0:T(8,128)(2,1)S(1)} %get-tuple-element.9.refs_1_, bf16[128,512]{1,0:T(8,128)(2,1)S(1)} %get-tuple-element.10.refs_2_, ...), custom_call_target="tpu_custom_call" | custom-call | bytes 1100000 | tf_op jit(solution)/shard_map/pallas_call | solution.py:669

commit v9 on v7

--- a/solution.py
+++ b/solution.py
@@ -232,6 +232,7 @@
     send(q_hbm.at[:, half(other)], q_two.at[mine], sib_recv.at[2], sibling)
     for h in (0, 1):
         send(kv_own.at[:, half(h)], kv_near.at[3 - 3 * core], near_recv.at[core], at(d, h), inside(sided=(1,)))
+    send(g_hbm.at[:, half(other)], g_two.at[mine], sib_recv.at[3], sibling)
     for h in (0, 1):
         send(
             pooled.at[:, half(h)], one_in.at[core * 2 + 1],
@@ -341,8 +342,6 @@
             two_in.at[side, pl.ds(0, 2)], two_in.at[side, pl.ds(2, 2)],
             two_recv.at[side, 2], at(sigma, core), inside(two, sigma),
         )
-
-    send(g_hbm.at[:, half(other)], g_two.at[mine], sib_recv.at[3], sibling)
 
     locals_in[4].wait()
     locals_in[6].wait()

time: 44.1 us -> 44.1 us (level)
  no operation moved by 1% of the time
where the time goes in v9:
time: 44.1 us; the launch traced here: 44 us
  Pallas kernels  43.4 us (98%)
  between operations  0.64 us (1%)
    pallas_call x1, Pallas kernels, body(): pl.pallas_call(kernel, out_shape=(out, out, out, out), in_specs=[pl.Block...  42.5 us

profile of v9, /device:TPU:6, one launch (start us, length us, event | category | flops | bytes accessed | tf_op | source)
XLA Modules:
  0.0 44.0 jit_solution(10230455898683865751)
XLA Ops:
  0.6 42.5 %shard_map.93 = (bf16[128,512]{1,0:T(8,128)(2,1)S(1)}, bf16[128,512]{1,0:T(8,128)(2,1)S(1)}, bf16[128,512]{1,0:T(8,128)(2,1)S(1)}, bf16[128,512]{1,0:T(8,128)(2,1)S(1)}) custom-call(bf16[128,512]{1,0:T(8,128)(2,1)} %q_hbm.1, bf16[128,512]{1,0:T(8,128)(2,1)} %k_hbm.1, bf16[128,512]{1,0:T(8,128)(2,1)} %v_hbm.1, bf16[128,512]{1,0:T(8,128)(2,1)} %g_hbm.1, ...), custom_call_target="tpu_custom_call" | custom-call | flops 700000000 | bytes 1100000 | tf_op jit(solution)/shard_map/pallas_call | solution.py:613
  43.2 0.8 %shard_map.94 = (bf16[128,512]{1,0:T(8,128)(2,1)}, bf16[128,512]{1,0:T(8,128)(2,1)}, bf16[128,512]{1,0:T(8,128)(2,1)}, bf16[128,512]{1,0:T(8,128)(2,1)}) custom-call(bf16[128,512]{1,0:T(8,128)(2,1)S(1)} %get-tuple-element.8.refs_0_, bf16[128,512]{1,0:T(8,128)(2,1)S(1)} %get-tuple-element.9.refs_1_, bf16[128,512]{1,0:T(8,128)(2,1)S(1)} %get-tuple-element.10.refs_2_, ...), custom_call_target="tpu_custom_call" | custom-call | bytes 1100000 | tf_op jit(solution)/shard_map/pallas_call | solution.py:668

commit v10 on v9

--- a/solution.py
+++ b/solution.py
@@ -424,7 +424,7 @@
             factors[h].append(jnp.exp2(highs[h][index] - highs[h][-1]) * inverse_totals[h])
             if part in (MIDDLE, LAST):
                 turned[h, part, :] = weight[h, :, part].astype(BF16).T
-    flush(keep=mates - 1)
+    forward_sends = len(started)
     for k in range(1, mates):
         source = (place + k) % mates
         arrived(stats.at[source], stat_recv.at[source])
@@ -547,6 +547,7 @@
             ).astype(BF16)
         send(near_out.at[b], near_back.at[core], back_near_recv.at[core], at(-direction(b), b), inside(-direction(b)))
 
+    flush(keep=len(started) - forward_sends)
     own = plain_backward(OWN, lambda h: own_of(0, h), lambda h: own_of(1, h))
     for kind in (0, 1):
         sib_out[kind * ROWS : (kind + 1) * ROWS] = jnp.where(core == 0, own[kind][second], own[kind][first]).astype(BF16)

time: 44.1 us -> 44.1 us (level)
  no operation moved by 1% of the time
where the time goes in v10:
time: 44.1 us; the launch traced here: 44 us
  Pallas kernels  43.4 us (98%)
  between operations  0.64 us (1%)
    pallas_call x1, Pallas kernels, body(): pl.pallas_call(kernel, out_shape=(out, out, out, out), in_specs=[pl.Block...  42.5 us

profile of v10, /device:TPU:6, one launch (start us, length us, event | category | flops | bytes accessed | tf_op | source)
XLA Modules:
  0.0 44.0 jit_solution(13114329248501923557)
XLA Ops:
  0.6 42.5 %shard_map.93 = (bf16[128,512]{1,0:T(8,128)(2,1)S(1)}, bf16[128,512]{1,0:T(8,128)(2,1)S(1)}, bf16[128,512]{1,0:T(8,128)(2,1)S(1)}, bf16[128,512]{1,0:T(8,128)(2,1)S(1)}) custom-call(bf16[128,512]{1,0:T(8,128)(2,1)} %q_hbm.1, bf16[128,512]{1,0:T(8,128)(2,1)} %k_hbm.1, bf16[128,512]{1,0:T(8,128)(2,1)} %v_hbm.1, bf16[128,512]{1,0:T(8,128)(2,1)} %g_hbm.1, ...), custom_call_target="tpu_custom_call" | custom-call | flops 700000000 | bytes 1100000 | tf_op jit(solution)/shard_map/pallas_call | solution.py:614
  43.2 0.8 %shard_map.94 = (bf16[128,512]{1,0:T(8,128)(2,1)}, bf16[128,512]{1,0:T(8,128)(2,1)}, bf16[128,512]{1,0:T(8,128)(2,1)}, bf16[128,512]{1,0:T(8,128)(2,1)}) custom-call(bf16[128,512]{1,0:T(8,128)(2,1)S(1)} %get-tuple-element.8.refs_0_, bf16[128,512]{1,0:T(8,128)(2,1)S(1)} %get-tuple-element.9.refs_1_, bf16[128,512]{1,0:T(8,128)(2,1)S(1)} %get-tuple-element.10.refs_2_, ...), custom_call_target="tpu_custom_call" | custom-call | bytes 1100000 | tf_op jit(solution)/shard_map/pallas_call | solution.py:669
